TPU v7x, 32 devices: a whole 2x2x4 slice. The times are simulated.
32 devices in a mesh: gx: 16 (over z, x, core), gy: 2 (over y).
Axes of the slice: x: 2, y: 2, z: 4, core: 2. Of those that a mesh axis runs over, the one named last changes fastest.
Arguments:
- orbitals: float32 [2, 32, 1024, 256], P(None, None, 'gx', 'gy'), may hold values from -12 to 12
- potential: float32 [32, 1024, 256], P(None, 'gx', 'gy'), may hold values from 0.5 to 2
- shift_ratio: float32 [1], replicated, may hold values from 16 to 48
Outputs:
- orbitals_next: float32 [2, 32, 1024, 256], P(None, None, 'gx', 'gy')
All inputs are finite; a program needn't handle non-finite values.
Results may differ from a plain program's by a relative error of at most 0.0003.
Values sent between devices are 32-bit elements; how exact they have to be, the bound alone decides.
A program may use at most 128 MiB of HBM per device.

v0:
```python
import functools

import jax
import jax.numpy as jnp
from jax import lax
from jax.experimental import pallas as pl
from jax.experimental.pallas import tpu as pltpu
from jax.sharding import PartitionSpec as P

TAU = 4.0
EPS = 1e-06
COUPLING_FIRST = 0.06
COUPLING_SECOND = 0.05
COUPLING_CROSS = 0.04
MESH = pl.DeviceIdType.MESH
LANES = 128


def wait_bytes(ref, sem):
    pltpu.make_async_copy(ref, ref, sem).wait()


def step_kernel(
    groups,
    owners,
    cells,
    params,
    orb_hbm,
    pot_hbm,
    out_hbm,
    ratio_ref,
    orb,
    pot,
    app,
    table,
    weights,
    x_send,
    x_halo,
    y_send,
    y_halo,
    tip_send,
    tip_recv,
    carry_send,
    carry,
    sums_send,
    sums_recv,
    mass_send,
    mass_recv,
    load_sem,
    halo_send_sem,
    halo_recv_sem,
    send_sem,
    recv_sem,
    out_sem,
):
    comps, levels, width, lanes = orb.shape
    per = levels // owners
    rows = comps * per
    devices = 2 * groups
    gx = lax.axis_index("gx")
    gy = lax.axis_index("gy")
    lane = lax.broadcasted_iota(jnp.int32, (width, lanes), 1)
    row = lax.broadcasted_iota(jnp.int32, (width, lanes), 0)
    lane_row = lax.broadcasted_iota(jnp.int32, (1, lanes), 1)

    def device_at(step):
        return (lax.rem(gx + step // 2, groups), lax.rem(gy + step % 2, 2))

    def slot_at(step):
        return lax.rem(groups - step // 2, groups) * 2 + step % 2

    load_orb = pltpu.make_async_copy(orb_hbm, orb, load_sem.at[0])
    load_pot = pltpu.make_async_copy(pot_hbm, pot, load_sem.at[1])
    load_orb.start()
    load_pot.start()

    barrier = pltpu.get_barrier_semaphore()

    def greet(step, _):
        pl.semaphore_signal(barrier, inc=1, device_id=device_at(step), device_id_type=MESH)
        return 0

    lax.fori_loop(1, devices, greet, 0)

    decay, gain, tip_gain, block, inv_wrap = (params[i] for i in range(5))
    position = row.astype(jnp.float32)
    weights[0] = jnp.exp(-decay * (float(width - 1) - position))
    weights[1] = jnp.exp(-decay * position)
    t_row = lax.broadcasted_iota(jnp.int32, (width, 3 * width), 0)
    t_col = lax.broadcasted_iota(jnp.int32, (width, 3 * width), 1)
    t_mod = jnp.where(t_col >= 2 * width, t_col - 2 * width, jnp.where(t_col >= width, t_col - width, t_col))
    green = gain * jnp.exp(-decay * jnp.abs(t_row - t_mod).astype(jnp.float32))
    high = green.astype(jnp.bfloat16)
    low = (green - high.astype(jnp.float32)).astype(jnp.bfloat16)
    table[...] = jnp.where(t_col >= 2 * width, low.astype(jnp.float32), high.astype(jnp.float32)).astype(jnp.bfloat16)

    load_orb.wait()

    def pack(z, held):
        for c in range(comps):
            plane = orb[c, z]
            index = z * comps + c
            held = jnp.where(lane // 2 == index, pltpu.roll(plane, 2 * index + 1, 1), held)
            x_send[0, pl.ds(index, 1), :] = orb[c, z, width - 1 : width, :]
            x_send[1, pl.ds(index, 1), :] = orb[c, z, 0:1, :]
        return held

    y_send[...] = lax.fori_loop(0, levels, pack, jnp.zeros((width, lanes), jnp.float32))

    pl.semaphore_wait(barrier, devices - 1)
    right = lax.rem(gx + 1, groups)
    left = lax.rem(gx + groups - 1, groups)
    halos = [
        pltpu.make_async_remote_copy(
            src, dst, halo_send_sem.at[i], halo_recv_sem.at[i], device_id=target, device_id_type=MESH
        )
        for i, (src, dst, target) in enumerate(
            (
                (y_send, y_halo, (gx, 1 - gy)),
                (x_send.at[0], x_halo.at[0], (right, gy)),
                (x_send.at[1], x_halo.at[1], (left, gy)),
            )
        )
    ]
    for copy in halos:
        copy.start()
    load_pot.wait()
    for copy in halos:
        copy.wait()

    lack = y_halo[...] - y_send[...]
    y_halo[...] = jnp.where(lane % 2 == 0, pltpu.roll(lack, lanes - 1, 1), pltpu.roll(lack, 1, 1))

    def fold(x):
        total = x[0:8]
        for i in range(8, width, 8):
            total = total + x[i : i + 8]
        return total

    def apply_level(z, owner, local, sums):
        o = [orb[c, z] for c in range(comps)]
        before = lax.rem(z + levels - 1, levels)
        after = lax.rem(z + 1, levels)
        squares = [x * x for x in o]
        density = (
            COUPLING_FIRST * squares[0] + COUPLING_CROSS * squares[1],
            COUPLING_CROSS * squares[0] + COUPLING_SECOND * squares[1],
        )
        trap = pot[z]
        result = []
        for c in range(comps):
            index = z * comps + c
            mine = o[c]
            ends = pltpu.roll(y_halo[...], lanes - 1 - 2 * index, 1)
            ends = jnp.where((lane == 0) | (lane == lanes - 1), ends, 0.0)
            prior = jnp.where(row == 0, x_halo[0, pl.ds(index, 1), :], pltpu.roll(mine, 1, 0))
            later = jnp.where(row == width - 1, x_halo[1, pl.ds(index, 1), :], pltpu.roll(mine, width - 1, 0))
            near = pltpu.roll(mine, 1, 1) + pltpu.roll(mine, lanes - 1, 1) + ends
            near = near + prior + later + orb[c, before] + orb[c, after]
            applied = -0.5 * (near - 6.0 * mine) + (trap + density[c]) * mine
            app[c, z] = applied
            for i, x in enumerate((applied, mine)):
                for j in range(2):
                    at = (2 * i + j) * rows + local * comps + c
                    tip_send[owner, at : at + 1, :] = jnp.sum(fold(weights[j] * x), axis=0, keepdims=True)
            result.append(sums[2 * c] + fold(mine * applied))
            result.append(sums[2 * c + 1] + fold(squares[c]))
        return tuple(result)

    def apply_owner(step, sums):
        owner = lax.rem(lax.rem(gx, owners) + 1 + step, owners)
        for local in range(per):
            sums = apply_level(owner * per + local, owner, local, sums)

        @pl.when(owner != gx)
        def _():
            pltpu.make_async_remote_copy(
                tip_send.at[owner],
                tip_recv.at[lax.rem(gx - owner + groups, groups)],
                send_sem.at[0],
                recv_sem.at[0],
                device_id=(owner, gy),
                device_id_type=MESH,
            ).start()

        return sums

    zero = jnp.zeros((8, lanes), jnp.float32)
    sums = lax.fori_loop(0, owners, apply_owner, (zero,) * (2 * comps))

    def lane_of(values):
        packed = jnp.zeros((1, lanes), jnp.float32)
        for i, x in enumerate(values):
            whole = jnp.sum(jnp.sum(x, axis=0, keepdims=True), axis=1, keepdims=True)
            packed = jnp.where(lane_row == i, whole, packed)
        return packed

    def spread(source, target, which):
        def send(step, _):
            pltpu.make_async_remote_copy(
                source.at[0],
                target.at[slot_at(step)],
                send_sem.at[which],
                recv_sem.at[which],
                device_id=device_at(step),
                device_id_type=MESH,
            ).start()
            return 0

        lax.fori_loop(1, devices, send, 0)

    def gathered(target, which, count):
        wait_bytes(target.at[pl.ds(1, devices - 1)], recv_sem.at[which])
        total = jnp.sum(target[...], axis=0)
        return [
            jnp.sum(jnp.where(lane_row == i, total, 0.0), axis=1, keepdims=True) for i in range(count)
        ]

    own = lane_of(sums)
    sums_send[0] = own
    sums_recv[0] = own
    spread(sums_send, sums_recv, 1)

    @pl.when(gx < owners)
    def _():
        tip_recv[0] = tip_send[lax.rem(gx, owners)]

    totals = gathered(sums_recv, 1, 2 * comps)
    mean_square = [totals[2 * c + 1] / cells for c in range(comps)]
    energy = [totals[2 * c] / cells / (mean_square[c] + EPS) for c in range(comps)]

    @pl.when(gx < owners)
    def _():
        wait_bytes(tip_recv.at[pl.ds(1, groups - 1)], recv_sem.at[0])
        tip_row = lax.broadcasted_iota(jnp.int32, (2 * rows, lanes), 0)
        scale = jnp.where(tip_row % 2 == 0, energy[0], energy[1])

        def tips(k):
            return tip_recv[k, 0 : 2 * rows, :] - scale * tip_recv[k, 2 * rows : 4 * rows, :]

        def collect(k, held):
            ahead, behind = held
            return block * ahead + tips(k), block * behind + tips(groups - 1 - k)

        start = jnp.zeros((2 * rows, lanes), jnp.float32)
        ahead, behind = lax.fori_loop(0, groups, collect, (start, start))

        def hand_out(k, held):
            ahead, behind = held
            back = groups - 1 - k
            carry_send[k, 0:rows, :] = ahead[0:rows]
            carry_send[back, rows : 2 * rows, :] = behind[rows : 2 * rows]
            return block * ahead + tip_gain * tips(k), block * behind + tip_gain * tips(back)

        factor = tip_gain * inv_wrap
        lax.fori_loop(0, groups, hand_out, (factor * ahead, factor * behind))

        def send(step, _):
            pltpu.make_async_remote_copy(
                carry_send.at[step],
                carry.at[gx],
                send_sem.at[2],
                recv_sem.at[2],
                device_id=(lax.rem(gx + step, groups), gy),
                device_id_type=MESH,
            ).start()
            return 0

        lax.fori_loop(1, groups, send, 0)
        carry[lax.rem(gx, owners)] = carry_send[0]

    def solve(z, _):
        pair = jnp.concatenate([app[c, z] - energy[c] * orb[c, z] for c in range(comps)], axis=1)
        high = pair.astype(jnp.bfloat16)
        low = (pair - high.astype(jnp.float32)).astype(jnp.bfloat16)
        local = jnp.dot(
            table[...], jnp.concatenate([high, low, high], axis=0), preferred_element_type=jnp.float32
        )
        for c in range(comps):
            app[c, z] = orb[c, z] - local[:, c * lanes : (c + 1) * lanes]
        return 0

    lax.fori_loop(0, levels, solve, 0, unroll=2)

    @pl.when(gx < owners)
    def _():
        wait_bytes(carry.at[pl.ds(0, owners - 1)], recv_sem.at[2])

    @pl.when(gx >= owners)
    def _():
        wait_bytes(carry, recv_sem.at[2])

    def update_owner(owner, masses):
        masses = list(masses)
        for local in range(per):
            z = owner * per + local
            for c in range(comps):
                at = local * comps + c
                update = app[c, z] - (
                    weights[1] * carry[owner, at : at + 1, :]
                    + weights[0] * carry[owner, rows + at : rows + at + 1, :]
                )
                app[c, z] = update
                masses[c] = masses[c] + fold(update * update)
        levels_here = pl.ds(owner * per, per)
        pltpu.make_async_copy(app.at[:, levels_here], out_hbm.at[:, levels_here], out_sem).start()
        return tuple(masses)

    masses = lax.fori_loop(0, owners, update_owner, (zero,) * comps)
    own = lane_of(masses)
    mass_send[0] = own
    mass_recv[0] = own
    spread(mass_send, mass_recv, 3)
    totals = gathered(mass_recv, 3, comps)
    for c in range(comps):
        ratio = jnp.sqrt(mean_square[c] / (totals[c] / cells + EPS))
        ratio_ref[c : c + 1, :] = jnp.broadcast_to(ratio, (1, lanes))

    @pl.when(gx < owners)
    def _():
        wait_bytes(tip_send.at[pl.ds(0, owners - 1)], send_sem.at[0])
        wait_bytes(carry_send.at[pl.ds(1, groups - 1)], send_sem.at[2])

    @pl.when(gx >= owners)
    def _():
        wait_bytes(tip_send, send_sem.at[0])

    wait_bytes(sums_recv.at[pl.ds(1, devices - 1)], send_sem.at[1])
    wait_bytes(mass_recv.at[pl.ds(1, devices - 1)], send_sem.at[3])
    pltpu.make_async_copy(app, out_hbm, out_sem).wait()


def shards(orbitals, potential, shift_ratio):
    groups = lax.axis_size("gx")
    columns = lax.axis_size("gy")
    comps, levels, width, lanes = orbitals.shape
    assert columns == 2 and lanes == LANES and 2 * comps * levels == lanes
    owners = min(groups, levels)
    rows = comps * (levels // owners)
    planes = comps * levels
    devices = groups * columns
    line_cells = width * groups
    cells = float(levels * line_cells * lanes * columns)
    sigma = shift_ratio[0] / float(line_cells * line_cells)
    decay = jnp.log1p(sigma + jnp.sqrt(sigma * (sigma + 2.0)))
    gain = TAU * jnp.tanh(0.5 * decay)
    params = jnp.stack(
        [
            decay,
            gain,
            gain * jnp.exp(-decay),
            jnp.exp(-decay * width),
            -1.0 / jnp.expm1(-decay * line_cells),
        ]
    )
    f32 = jnp.float32
    update, ratio = pl.pallas_call(
        functools.partial(step_kernel, groups, owners, cells),
        out_shape=(
            jax.ShapeDtypeStruct(orbitals.shape, f32),
            jax.ShapeDtypeStruct((comps, lanes), f32),
        ),
        in_specs=[
            pl.BlockSpec(memory_space=pltpu.SMEM),
            pl.BlockSpec(memory_space=pl.ANY),
            pl.BlockSpec(memory_space=pl.ANY),
        ],
        out_specs=(
            pl.BlockSpec(memory_space=pl.ANY),
            pl.BlockSpec(memory_space=pltpu.VMEM),
        ),
        scratch_shapes=[
            pltpu.VMEM(orbitals.shape, f32),
            pltpu.VMEM(potential.shape, f32),
            pltpu.VMEM(orbitals.shape, f32),
            pltpu.VMEM((width, 3 * width), jnp.bfloat16),
            pltpu.VMEM((2, width, lanes), f32),
            pltpu.VMEM((2, planes, lanes), f32),
            pltpu.VMEM((2, planes, lanes), f32),
            pltpu.VMEM((width, lanes), f32),
            pltpu.VMEM((width, lanes), f32),
            pltpu.VMEM((owners, 4 * rows, lanes), f32),
            pltpu.VMEM((groups, 4 * rows, lanes), f32),
            pltpu.VMEM((groups, 2 * rows, lanes), f32),
            pltpu.VMEM((owners, 2 * rows, lanes), f32),
            pltpu.VMEM((1, 1, lanes), f32),
            pltpu.VMEM((devices, 1, lanes), f32),
            pltpu.VMEM((1, 1, lanes), f32),
            pltpu.VMEM((devices, 1, lanes), f32),
            pltpu.SemaphoreType.DMA((2,)),
            pltpu.SemaphoreType.DMA((3,)),
            pltpu.SemaphoreType.DMA((3,)),
            pltpu.SemaphoreType.DMA((4,)),
            pltpu.SemaphoreType.DMA((4,)),
            pltpu.SemaphoreType.DMA,
        ],
        compiler_params=pltpu.CompilerParams(
            collective_id=0, has_side_effects=True, vmem_limit_bytes=32 * 1024 * 1024
        ),
        name="power_step",
    )(params, orbitals, potential)
    return update * ratio[:, None, None, :]


def solution(mesh):
    in_specs = (P(None, None, "gx", "gy"), P(None, "gx", "gy"), P())
    out_specs = P(None, None, "gx", "gy")
    return jax.shard_map(shards, mesh=mesh, in_specs=in_specs, out_specs=out_specs, check_vma=False)
```

profile of v0, /device:TPU:0, one launch (start us, length us, event | category | flops | bytes accessed | tf_op | source)
XLA Modules:
  0.0 35.8 jit_solution(2672521739517279721)
XLA Ops:
  0.9 0.1 stack.23.params
  1.0 0.0 copy-start
  1.0 1.6 %copy-done = f32[2,32,64,128]{3,2,1,0:T(8,128)S(1)} copy-done((f32[2,32,64,128]{3,2,1,0:T(8,128)S(1)}, f32[2,32,64,128]{3,2,1,0:T(8,128)}, u32[]{:S(2)}) %copy-start) | copy-done | bytes 2097176
  2.6 0.0 copy-start.1
  2.6 1.2 %copy-done.1 = f32[32,64,128]{2,1,0:T(8,128)S(1)} copy-done((f32[32,64,128]{2,1,0:T(8,128)S(1)}, f32[32,64,128]{2,1,0:T(8,128)}, u32[]{:S(2)}) %copy-start.1) | copy-done | bytes 1048600
  3.8 30.4 %power_step.1 = (f32[2,32,64,128]{3,2,1,0:T(8,128)S(1)}, f32[2,128]{1,0:T(2,128)S(1)}) custom-call(f32[5]{0:T(128)S(1)} %stack.23.params, f32[2,32,64,128]{3,2,1,0:T(8,128)S(1)} %copy-done, f32[32,64,128]{2,1,0:T(8,128)S(1)} %copy-done.1), custom_call_target="tpu_custom_call" | custom-call | tf_op jit(solution)/shard_map/power_step/pallas_call | solution.py:357
  34.3 1.6 %broadcast_multiply_fusion = f32[2,32,64,128]{3,2,1,0:T(8,128)} fusion(f32[2,32,64,128]{3,2,1,0:T(8,128)S(1)} %get-tuple-element.7, f32[2,128]{1,0:T(2,128)S(1)} %get-tuple-element.8), kind=kLoop, calls=%fused_computation | loop fusion | flops 524288 | bytes 4195328 | tf_op jit(solution)/shard_map/mul | solution.py:402
Async XLA Ops:
  1.0 1.6 %copy-start = (f32[2,32,64,128]{3,2,1,0:T(8,128)S(1)}, f32[2,32,64,128]{3,2,1,0:T(8,128)}, u32[]{:S(2)}) copy-start(f32[2,32,64,128]{3,2,1,0:T(8,128)} %orb_hbm.1) | copy-start | bytes 6291460
  2.6 1.2 %copy-start.1 = (f32[32,64,128]{2,1,0:T(8,128)S(1)}, f32[32,64,128]{2,1,0:T(8,128)}, u32[]{:S(2)}) copy-start(f32[32,64,128]{2,1,0:T(8,128)} %pot_hbm.1) | copy-start | bytes 3145732
where the time goes:
time: 36 us; the launch traced here: 35.8 us
  Pallas kernels  30.4 us (84%)
  local copies, waits for them, and re-layouts  2.9 us (8%)
  other arithmetic  1.55 us (4%)
  between operations  0.96 us (3%)
    pallas_call x1, Pallas kernels, shards(): pl.pallas_call(functools.partial(step_kernel, groups, owners, cells), out...  30.4 us
    unnamed x4, local copies, waits for them, and re-layouts  2.82 us
    mul x1, other arithmetic, shards(): return update * ratio[:, None, None, :]  1.55 us

commit v1 on v0

--- a/solution.py
+++ b/solution.py
@@ -14,6 +14,7 @@
 COUPLING_CROSS = 0.04
 MESH = pl.DeviceIdType.MESH
 LANES = 128
+CHUNKS = 4
 
 
 def wait_bytes(ref, sem):
@@ -32,12 +33,14 @@
     orb,
     pot,
     app,
+    shift,
     table,
     weights,
     x_send,
     x_halo,
     y_send,
     y_halo,
+    tips_ref,
     tip_send,
     tip_recv,
     carry_send,
@@ -55,6 +58,7 @@
 ):
     comps, levels, width, lanes = orb.shape
     per = levels // owners
+    early = shift.shape[1]
     rows = comps * per
     devices = 2 * groups
     gx = lax.axis_index("gx")
@@ -63,26 +67,35 @@
     row = lax.broadcasted_iota(jnp.int32, (width, lanes), 0)
     lane_row = lax.broadcasted_iota(jnp.int32, (1, lanes), 1)
 
-    def device_at(step):
-        return (lax.rem(gx + step // 2, groups), lax.rem(gy + step % 2, 2))
-
-    def slot_at(step):
-        return lax.rem(groups - step // 2, groups) * 2 + step % 2
-
-    load_orb = pltpu.make_async_copy(orb_hbm, orb, load_sem.at[0])
-    load_pot = pltpu.make_async_copy(pot_hbm, pot, load_sem.at[1])
-    load_orb.start()
-    load_pot.start()
+    def peer(step):
+        other = gx + step
+        return jnp.where(other >= groups, other - groups, other)
+
+    def device_at(step, side):
+        return (peer(step), gy if side == 0 else 1 - gy)
+
+    chunk = levels // CHUNKS
+    loads = [
+        pltpu.make_async_copy(
+            orb_hbm.at[:, pl.ds(i * chunk, chunk)], orb.at[:, pl.ds(i * chunk, chunk)], load_sem.at[i]
+        )
+        for i in range(CHUNKS)
+    ]
+    loads.append(pltpu.make_async_copy(pot_hbm, pot, load_sem.at[CHUNKS]))
+    for copy in loads:
+        copy.start()
 
     barrier = pltpu.get_barrier_semaphore()
 
     def greet(step, _):
-        pl.semaphore_signal(barrier, inc=1, device_id=device_at(step), device_id_type=MESH)
+        for side in range(2):
+            pl.semaphore_signal(barrier, inc=1, device_id=device_at(step, side), device_id_type=MESH)
         return 0
 
-    lax.fori_loop(1, devices, greet, 0)
-
-    decay, gain, tip_gain, block, inv_wrap = (params[i] for i in range(5))
+    pl.semaphore_signal(barrier, inc=1, device_id=(gx, 1 - gy), device_id_type=MESH)
+    lax.fori_loop(1, groups, greet, 0)
+
+    decay, gain, tip_gain, block, inv_wrap, edge = (params[i] for i in range(6))
     position = row.astype(jnp.float32)
     weights[0] = jnp.exp(-decay * (float(width - 1) - position))
     weights[1] = jnp.exp(-decay * position)
@@ -94,8 +107,6 @@
     low = (green - high.astype(jnp.float32)).astype(jnp.bfloat16)
     table[...] = jnp.where(t_col >= 2 * width, low.astype(jnp.float32), high.astype(jnp.float32)).astype(jnp.bfloat16)
 
-    load_orb.wait()
-
     def pack(z, held):
         for c in range(comps):
             plane = orb[c, z]
@@ -105,11 +116,13 @@
             x_send[1, pl.ds(index, 1), :] = orb[c, z, 0:1, :]
         return held
 
-    y_send[...] = lax.fori_loop(0, levels, pack, jnp.zeros((width, lanes), jnp.float32))
+    held = jnp.zeros((width, lanes), jnp.float32)
+    for i in range(CHUNKS):
+        loads[i].wait()
+        held = lax.fori_loop(i * chunk, (i + 1) * chunk, pack, held, unroll=2)
+    y_send[...] = held
 
     pl.semaphore_wait(barrier, devices - 1)
-    right = lax.rem(gx + 1, groups)
-    left = lax.rem(gx + groups - 1, groups)
     halos = [
         pltpu.make_async_remote_copy(
             src, dst, halo_send_sem.at[i], halo_recv_sem.at[i], device_id=target, device_id_type=MESH
@@ -117,19 +130,14 @@
         for i, (src, dst, target) in enumerate(
             (
                 (y_send, y_halo, (gx, 1 - gy)),
-                (x_send.at[0], x_halo.at[0], (right, gy)),
-                (x_send.at[1], x_halo.at[1], (left, gy)),
+                (x_send.at[0], x_halo.at[0], (peer(1), gy)),
+                (x_send.at[1], x_halo.at[1], (peer(groups - 1), gy)),
             )
         )
     ]
     for copy in halos:
         copy.start()
-    load_pot.wait()
-    for copy in halos:
-        copy.wait()
-
-    lack = y_halo[...] - y_send[...]
-    y_halo[...] = jnp.where(lane % 2 == 0, pltpu.roll(lack, lanes - 1, 1), pltpu.roll(lack, 1, 1))
+    loads[CHUNKS].wait()
 
     def fold(x):
         total = x[0:8]
@@ -137,7 +145,7 @@
             total = total + x[i : i + 8]
         return total
 
-    def apply_level(z, owner, local, sums):
+    def apply_level(z, sums):
         o = [orb[c, z] for c in range(comps)]
         before = lax.rem(z + levels - 1, levels)
         after = lax.rem(z + 1, levels)
@@ -146,31 +154,89 @@
             COUPLING_FIRST * squares[0] + COUPLING_CROSS * squares[1],
             COUPLING_CROSS * squares[0] + COUPLING_SECOND * squares[1],
         )
-        trap = pot[z]
+        trap = pot[z] + 3.0
         result = []
         for c in range(comps):
-            index = z * comps + c
             mine = o[c]
-            ends = pltpu.roll(y_halo[...], lanes - 1 - 2 * index, 1)
-            ends = jnp.where((lane == 0) | (lane == lanes - 1), ends, 0.0)
-            prior = jnp.where(row == 0, x_halo[0, pl.ds(index, 1), :], pltpu.roll(mine, 1, 0))
-            later = jnp.where(row == width - 1, x_halo[1, pl.ds(index, 1), :], pltpu.roll(mine, width - 1, 0))
-            near = pltpu.roll(mine, 1, 1) + pltpu.roll(mine, lanes - 1, 1) + ends
-            near = near + prior + later + orb[c, before] + orb[c, after]
-            applied = -0.5 * (near - 6.0 * mine) + (trap + density[c]) * mine
+            near = pltpu.roll(mine, 1, 1) + pltpu.roll(mine, lanes - 1, 1)
+            near = near + pltpu.roll(mine, 1, 0) + pltpu.roll(mine, width - 1, 0)
+            near = near + orb[c, before] + orb[c, after]
+            applied = (trap + density[c]) * mine - 0.5 * near
             app[c, z] = applied
             for i, x in enumerate((applied, mine)):
                 for j in range(2):
-                    at = (2 * i + j) * rows + local * comps + c
-                    tip_send[owner, at : at + 1, :] = jnp.sum(fold(weights[j] * x), axis=0, keepdims=True)
+                    tip = jnp.sum(fold(weights[j] * x), axis=0, keepdims=True)
+                    tips_ref[2 * i + j, pl.ds(z * comps + c, 1), :] = tip
             result.append(sums[2 * c] + fold(mine * applied))
             result.append(sums[2 * c + 1] + fold(squares[c]))
         return tuple(result)
 
-    def apply_owner(step, sums):
-        owner = lax.rem(lax.rem(gx, owners) + 1 + step, owners)
-        for local in range(per):
-            sums = apply_level(owner * per + local, owner, local, sums)
+    zero = jnp.zeros((8, lanes), jnp.float32)
+    sums = list(lax.fori_loop(0, levels, apply_level, (zero,) * (2 * comps), unroll=2))
+
+    for copy in halos:
+        copy.wait()
+    lack = y_halo[...] - y_send[...]
+    lack = jnp.where(lane % 2 == 0, pltpu.roll(lack, lanes - 1, 1), pltpu.roll(lack, 1, 1))
+    y_halo[...] = lack
+    x_lack = [x_halo[j] - x_send[j] for j in range(2)]
+    for j in range(2):
+        x_halo[j] = x_lack[j]
+    x_cross = x_send[1] * x_lack[0] + x_send[0] * x_lack[1]
+    y_cross = y_send[...] * lack
+    for c in range(comps):
+        more = jnp.where(row % comps == c, x_cross, 0.0) + jnp.where(lane // 2 % comps == c, y_cross, 0.0)
+        sums[2 * c] = sums[2 * c] - 0.5 * fold(more)
+    for j in range(2):
+        ends = jnp.sum(fold(weights[j] * lack), axis=0, keepdims=True)
+        last = jnp.sum(jnp.where(lane == 2 * row, ends, 0.0), axis=1, keepdims=True)
+        first = jnp.sum(jnp.where(lane == 2 * row + 1, ends, 0.0), axis=1, keepdims=True)
+        more = jnp.where(lane == 0, first, jnp.where(lane == lanes - 1, last, 0.0))
+        more = more + x_lack[1 - j] + edge * x_lack[j]
+        tips_ref[j] = tips_ref[j] - 0.5 * more
+
+    def lane_of(values):
+        packed = jnp.zeros((1, lanes), jnp.float32)
+        for i, x in enumerate(values):
+            whole = jnp.sum(jnp.sum(x, axis=0, keepdims=True), axis=1, keepdims=True)
+            packed = jnp.where(lane_row == i, whole, packed)
+        return packed
+
+    def spread(source, target, which):
+        def copy_to(slot, device):
+            pltpu.make_async_remote_copy(
+                source.at[0],
+                target.at[slot],
+                send_sem.at[which],
+                recv_sem.at[which],
+                device_id=device,
+                device_id_type=MESH,
+            ).start()
+
+        def send(step, _):
+            for side in range(2):
+                copy_to(2 * (groups - step) + side, device_at(step, side))
+            return 0
+
+        copy_to(1, (gx, 1 - gy))
+        lax.fori_loop(1, groups, send, 0)
+
+    def gathered(target, which, count):
+        wait_bytes(target.at[pl.ds(1, devices - 1)], recv_sem.at[which])
+        total = jnp.sum(target[...], axis=0)
+        return [
+            jnp.sum(jnp.where(lane_row == i, total, 0.0), axis=1, keepdims=True) for i in range(count)
+        ]
+
+    own = lane_of(sums)
+    sums_send[0] = own
+    sums_recv[0] = own
+    spread(sums_send, sums_recv, 1)
+
+    def send_tips(step, _):
+        owner = lax.rem(gx + 1 + step, owners)
+        for q in range(4):
+            tip_send[owner, q * rows : (q + 1) * rows, :] = tips_ref[q, pl.ds(owner * rows, rows), :]
 
         @pl.when(owner != gx)
         def _():
@@ -183,47 +249,40 @@
                 device_id_type=MESH,
             ).start()
 
-        return sums
-
-    zero = jnp.zeros((8, lanes), jnp.float32)
-    sums = lax.fori_loop(0, owners, apply_owner, (zero,) * (2 * comps))
-
-    def lane_of(values):
-        packed = jnp.zeros((1, lanes), jnp.float32)
-        for i, x in enumerate(values):
-            whole = jnp.sum(jnp.sum(x, axis=0, keepdims=True), axis=1, keepdims=True)
-            packed = jnp.where(lane_row == i, whole, packed)
-        return packed
-
-    def spread(source, target, which):
-        def send(step, _):
-            pltpu.make_async_remote_copy(
-                source.at[0],
-                target.at[slot_at(step)],
-                send_sem.at[which],
-                recv_sem.at[which],
-                device_id=device_at(step),
-                device_id_type=MESH,
-            ).start()
-            return 0
-
-        lax.fori_loop(1, devices, send, 0)
-
-    def gathered(target, which, count):
-        wait_bytes(target.at[pl.ds(1, devices - 1)], recv_sem.at[which])
-        total = jnp.sum(target[...], axis=0)
-        return [
-            jnp.sum(jnp.where(lane_row == i, total, 0.0), axis=1, keepdims=True) for i in range(count)
-        ]
-
-    own = lane_of(sums)
-    sums_send[0] = own
-    sums_recv[0] = own
-    spread(sums_send, sums_recv, 1)
+        return 0
+
+    lax.fori_loop(0, owners, send_tips, 0)
 
     @pl.when(gx < owners)
     def _():
         tip_recv[0] = tip_send[lax.rem(gx, owners)]
+
+    def split_dot(fields):
+        wide = jnp.concatenate(fields, axis=1)
+        high = wide.astype(jnp.bfloat16)
+        low = (wide - high.astype(jnp.float32)).astype(jnp.bfloat16)
+        local = jnp.dot(
+            table[...], jnp.concatenate([high, low, high], axis=0), preferred_element_type=jnp.float32
+        )
+        return [local[:, i * lanes : (i + 1) * lanes] for i in range(len(fields))]
+
+    def whole_applied(c, z):
+        index = z * comps + c
+        ends = pltpu.roll(y_halo[...], lanes - 1 - 2 * index, 1)
+        ends = jnp.where((lane == 0) | (lane == lanes - 1), ends, 0.0)
+        ends = ends + jnp.where(row == 0, x_halo[0, pl.ds(index, 1), :], 0.0)
+        ends = ends + jnp.where(row == width - 1, x_halo[1, pl.ds(index, 1), :], 0.0)
+        return app[c, z] - 0.5 * ends
+
+    def solve_early(z, _):
+        o = [orb[c, z] for c in range(comps)]
+        local = split_dot([whole_applied(c, z) for c in range(comps)] + o)
+        for c in range(comps):
+            app[c, z] = o[c] - local[c]
+            shift[c, z] = local[comps + c]
+        return 0
+
+    lax.fori_loop(0, early, solve_early, 0, unroll=2)
 
     totals = gathered(sums_recv, 1, 2 * comps)
     mean_square = [totals[2 * c + 1] / cells for c in range(comps)]
@@ -261,7 +320,7 @@
                 carry.at[gx],
                 send_sem.at[2],
                 recv_sem.at[2],
-                device_id=(lax.rem(gx + step, groups), gy),
+                device_id=(peer(step), gy),
                 device_id_type=MESH,
             ).start()
             return 0
@@ -269,18 +328,14 @@
         lax.fori_loop(1, groups, send, 0)
         carry[lax.rem(gx, owners)] = carry_send[0]
 
-    def solve(z, _):
-        pair = jnp.concatenate([app[c, z] - energy[c] * orb[c, z] for c in range(comps)], axis=1)
-        high = pair.astype(jnp.bfloat16)
-        low = (pair - high.astype(jnp.float32)).astype(jnp.bfloat16)
-        local = jnp.dot(
-            table[...], jnp.concatenate([high, low, high], axis=0), preferred_element_type=jnp.float32
-        )
+    def solve_late(z, _):
+        o = [orb[c, z] for c in range(comps)]
+        local = split_dot([whole_applied(c, z) - energy[c] * o[c] for c in range(comps)])
         for c in range(comps):
-            app[c, z] = orb[c, z] - local[:, c * lanes : (c + 1) * lanes]
+            app[c, z] = o[c] - local[c]
         return 0
 
-    lax.fori_loop(0, levels, solve, 0, unroll=2)
+    lax.fori_loop(early, levels, solve_late, 0, unroll=2)
 
     @pl.when(gx < owners)
     def _():
@@ -290,13 +345,16 @@
     def _():
         wait_bytes(carry, recv_sem.at[2])
 
-    def update_owner(owner, masses):
+    def update_owner(is_early, owner, masses):
         masses = list(masses)
         for local in range(per):
             z = owner * per + local
             for c in range(comps):
                 at = local * comps + c
-                update = app[c, z] - (
+                update = app[c, z]
+                if is_early:
+                    update = update + energy[c] * shift[c, z]
+                update = update - (
                     weights[1] * carry[owner, at : at + 1, :]
                     + weights[0] * carry[owner, rows + at : rows + at + 1, :]
                 )
@@ -306,7 +364,8 @@
         pltpu.make_async_copy(app.at[:, levels_here], out_hbm.at[:, levels_here], out_sem).start()
         return tuple(masses)
 
-    masses = lax.fori_loop(0, owners, update_owner, (zero,) * comps)
+    masses = lax.fori_loop(0, early // per, functools.partial(update_owner, True), (zero,) * comps)
+    masses = lax.fori_loop(early // per, owners, functools.partial(update_owner, False), masses)
     own = lane_of(masses)
     mass_send[0] = own
     mass_recv[0] = own
@@ -335,8 +394,10 @@
     columns = lax.axis_size("gy")
     comps, levels, width, lanes = orbitals.shape
     assert columns == 2 and lanes == LANES and 2 * comps * levels == lanes
+    assert comps * levels == width
     owners = min(groups, levels)
     rows = comps * (levels // owners)
+    early = levels // 2
     planes = comps * levels
     devices = groups * columns
     line_cells = width * groups
@@ -351,6 +412,7 @@
             gain * jnp.exp(-decay),
             jnp.exp(-decay * width),
             -1.0 / jnp.expm1(-decay * line_cells),
+            jnp.exp(-decay * (width - 1)),
         ]
     )
     f32 = jnp.float32
@@ -373,12 +435,14 @@
             pltpu.VMEM(orbitals.shape, f32),
             pltpu.VMEM(potential.shape, f32),
             pltpu.VMEM(orbitals.shape, f32),
+            pltpu.VMEM((comps, early, width, lanes), f32),
             pltpu.VMEM((width, 3 * width), jnp.bfloat16),
             pltpu.VMEM((2, width, lanes), f32),
             pltpu.VMEM((2, planes, lanes), f32),
             pltpu.VMEM((2, planes, lanes), f32),
             pltpu.VMEM((width, lanes), f32),
             pltpu.VMEM((width, lanes), f32),
+            pltpu.VMEM((4, planes, lanes), f32),
             pltpu.VMEM((owners, 4 * rows, lanes), f32),
             pltpu.VMEM((groups, 4 * rows, lanes), f32),
             pltpu.VMEM((groups, 2 * rows, lanes), f32),
@@ -387,7 +451,7 @@
             pltpu.VMEM((devices, 1, lanes), f32),
             pltpu.VMEM((1, 1, lanes), f32),
             pltpu.VMEM((devices, 1, lanes), f32),
-            pltpu.SemaphoreType.DMA((2,)),
+            pltpu.SemaphoreType.DMA((CHUNKS + 1,)),
             pltpu.SemaphoreType.DMA((3,)),
             pltpu.SemaphoreType.DMA((3,)),
             pltpu.SemaphoreType.DMA((4,)),
@@ -395,7 +459,7 @@
             pltpu.SemaphoreType.DMA,
         ],
         compiler_params=pltpu.CompilerParams(
-            collective_id=0, has_side_effects=True, vmem_limit_bytes=32 * 1024 * 1024
+            collective_id=0, has_side_effects=True
         ),
         name="power_step",
     )(params, orbitals, potential)

time: 36 us -> 31.3 us (0.87)
  Pallas kernels: 30.4 us -> 26.3 us
  local copies, waits for them, and re-layouts: 2.9 us -> 0.61 us
  other arithmetic: 1.55 us -> 3.21 us
    pallas_call x1, Pallas kernels: 30.4 us -> 26.3 us  [shards(): pl.pallas_call(functools.partial(step_kernel, groups, owners, cells), out...]
    unnamed x4 -> x0, local copies, waits for them, and re-layouts: 2.82 us -> none
    mul x1, other arithmetic: 1.55 us -> 3.21 us  [shards(): return update * ratio[:, None, None, :]]
    another operation x1, local copies, waits for them, and re-layouts: 0.08 us -> 0.61 us  [shards(): jnp.stack([decay, gain, gain * jnp.exp(-decay), jnp.exp(-decay * width),...]
where the time goes in v1:
time: 31.3 us; the launch traced here: 31.1 us
  Pallas kernels  26.3 us (84%)
  other arithmetic  3.21 us (10%)
  between operations  1 us (3%)
  local copies, waits for them, and re-layouts  0.61 us (2%)
    pallas_call x1, Pallas kernels, shards(): pl.pallas_call(functools.partial(step_kernel, groups, owners, cells), out...  26.3 us
    mul x1, other arithmetic, shards(): return update * ratio[:, None, None, :]  3.21 us

profile of v1, /device:TPU:0, one launch (start us, length us, event | category | flops | bytes accessed | tf_op | source)
XLA Modules:
  0.0 31.1 jit_solution(16093199524750409732)
XLA Ops:
  1.0 0.6 %stack.27.params = f32[6]{0:T(128)} concatenate(f32[1]{0:T(128)} %bitcast.1, f32[1]{0:T(128)} %bitcast.2, f32[1]{0:T(128)} %bitcast.3, f32[1]{0:T(128)} %bitcast.4, f32[1]{0:T(128)} %bitcast.5, f32[1]{0:T(128)} %bitcast.6), dimensions={0} | concatenate | bytes 48 | tf_op jit(solution)/shard_map/stack | solution.py:408
  1.6 26.3 %power_step.1 = (f32[2,32,64,128]{3,2,1,0:T(8,128)}, f32[2,128]{1,0:T(2,128)}) custom-call(f32[6]{0:T(128)} %stack.27.params, f32[2,32,64,128]{3,2,1,0:T(8,128)} %orb_hbm.1, f32[32,64,128]{2,1,0:T(8,128)} %pot_hbm.1), custom_call_target="tpu_custom_call" | custom-call | tf_op jit(solution)/shard_map/power_step/pallas_call | solution.py:419
  27.9 3.2 %broadcast_multiply_fusion = f32[2,32,64,128]{3,2,1,0:T(8,128)} fusion(f32[2,32,64,128]{3,2,1,0:T(8,128)} %get-tuple-element.7, f32[2,128]{1,0:T(2,128)} %get-tuple-element.8), kind=kLoop, calls=%fused_computation | loop fusion | flops 524288 | bytes 4195328 | tf_op jit(solution)/shard_map/mul | solution.py:466

commit v2 on v1

--- a/solution.py
+++ b/solution.py
@@ -25,7 +25,7 @@
     groups,
     owners,
     cells,
-    params,
+    shift_ratio,
     orb_hbm,
     pot_hbm,
     out_hbm,
@@ -41,6 +41,7 @@
     y_send,
     y_halo,
     tips_ref,
+    moments,
     tip_send,
     tip_recv,
     carry_send,
@@ -95,14 +96,27 @@
     pl.semaphore_signal(barrier, inc=1, device_id=(gx, 1 - gy), device_id_type=MESH)
     lax.fori_loop(1, groups, greet, 0)
 
-    decay, gain, tip_gain, block, inv_wrap, edge = (params[i] for i in range(6))
+    line_cells = width * groups
+    sigma_wide = jnp.full((1, 2 * lanes), shift_ratio[0] / float(line_cells * line_cells), jnp.float32)
+    decay_wide = jnp.log1p(sigma_wide + jnp.sqrt(sigma_wide * (sigma_wide + 2.0)))
+    gain_wide = TAU * jnp.sqrt(sigma_wide / (sigma_wide + 2.0))
+    sigma, decay, gain = (x[:, :lanes] for x in (sigma_wide, decay_wide, gain_wide))
+    tip_gain = gain * jnp.exp(-decay)
+    block = jnp.exp(-decay * float(width))
+    inv_wrap = 1.0 / (1.0 - jnp.exp(-decay * float(line_cells)))
+    edge = jnp.exp(-decay * float(width - 1))
+    eight = jnp.exp(-8.0 * decay)
+    keep = 1.0 - TAU * sigma
     position = row.astype(jnp.float32)
     weights[0] = jnp.exp(-decay * (float(width - 1) - position))
     weights[1] = jnp.exp(-decay * position)
+    near_last = weights[0, width - 8 : width, :]
+    near_first = weights[1, 0:8, :]
     t_row = lax.broadcasted_iota(jnp.int32, (width, 3 * width), 0)
     t_col = lax.broadcasted_iota(jnp.int32, (width, 3 * width), 1)
     t_mod = jnp.where(t_col >= 2 * width, t_col - 2 * width, jnp.where(t_col >= width, t_col - width, t_col))
-    green = gain * jnp.exp(-decay * jnp.abs(t_row - t_mod).astype(jnp.float32))
+    distance = jnp.abs(t_row - t_mod).astype(jnp.float32)
+    green = gain_wide[:, : 3 * width] * jnp.exp(-decay_wide[:, : 3 * width] * distance)
     high = green.astype(jnp.bfloat16)
     low = (green - high.astype(jnp.float32)).astype(jnp.bfloat16)
     table[...] = jnp.where(t_col >= 2 * width, low.astype(jnp.float32), high.astype(jnp.float32)).astype(jnp.bfloat16)
@@ -119,7 +133,7 @@
     held = jnp.zeros((width, lanes), jnp.float32)
     for i in range(CHUNKS):
         loads[i].wait()
-        held = lax.fori_loop(i * chunk, (i + 1) * chunk, pack, held, unroll=2)
+        held = lax.fori_loop(i * chunk, (i + 1) * chunk, pack, held, unroll=4)
     y_send[...] = held
 
     pl.semaphore_wait(barrier, devices - 1)
@@ -130,8 +144,7 @@
         for i, (src, dst, target) in enumerate(
             (
                 (y_send, y_halo, (gx, 1 - gy)),
-                (x_send.at[0], x_halo.at[0], (peer(1), gy)),
-                (x_send.at[1], x_halo.at[1], (peer(groups - 1), gy)),
+                (x_send.at[1], x_halo, (peer(groups - 1), gy)),
             )
         )
     ]
@@ -144,6 +157,17 @@
         for i in range(8, width, 8):
             total = total + x[i : i + 8]
         return total
+
+    def weighted(x):
+        parts = [x[i : i + 8] for i in range(0, width, 8)]
+        to_last, to_first = parts[0], parts[-1]
+        for i in range(1, len(parts)):
+            to_last = to_last * eight + parts[i]
+            to_first = to_first * eight + parts[-1 - i]
+        return (
+            jnp.sum(to_last * near_last, axis=0, keepdims=True),
+            jnp.sum(to_first * near_first, axis=0, keepdims=True),
+        )
 
     def apply_level(z, sums):
         o = [orb[c, z] for c in range(comps)]
@@ -154,20 +178,19 @@
             COUPLING_FIRST * squares[0] + COUPLING_CROSS * squares[1],
             COUPLING_CROSS * squares[0] + COUPLING_SECOND * squares[1],
         )
-        trap = pot[z] + 3.0
+        trap = pot[z] + 2.0
         result = []
         for c in range(comps):
             mine = o[c]
             near = pltpu.roll(mine, 1, 1) + pltpu.roll(mine, lanes - 1, 1)
-            near = near + pltpu.roll(mine, 1, 0) + pltpu.roll(mine, width - 1, 0)
             near = near + orb[c, before] + orb[c, after]
             applied = (trap + density[c]) * mine - 0.5 * near
             app[c, z] = applied
             for i, x in enumerate((applied, mine)):
-                for j in range(2):
-                    tip = jnp.sum(fold(weights[j] * x), axis=0, keepdims=True)
+                for j, tip in enumerate(weighted(x)):
                     tips_ref[2 * i + j, pl.ds(z * comps + c, 1), :] = tip
-            result.append(sums[2 * c] + fold(mine * applied))
+            along = mine - pltpu.roll(mine, width - 1, 0)
+            result.append(sums[2 * c] + fold(mine * (applied + along)))
             result.append(sums[2 * c + 1] + fold(squares[c]))
         return tuple(result)
 
@@ -179,20 +202,16 @@
     lack = y_halo[...] - y_send[...]
     lack = jnp.where(lane % 2 == 0, pltpu.roll(lack, lanes - 1, 1), pltpu.roll(lack, 1, 1))
     y_halo[...] = lack
-    x_lack = [x_halo[j] - x_send[j] for j in range(2)]
-    for j in range(2):
-        x_halo[j] = x_lack[j]
-    x_cross = x_send[1] * x_lack[0] + x_send[0] * x_lack[1]
+    x_cross = x_send[0] * (x_halo[...] - x_send[1])
     y_cross = y_send[...] * lack
     for c in range(comps):
-        more = jnp.where(row % comps == c, x_cross, 0.0) + jnp.where(lane // 2 % comps == c, y_cross, 0.0)
-        sums[2 * c] = sums[2 * c] - 0.5 * fold(more)
+        sums[2 * c] = sums[2 * c] - fold(jnp.where(row % comps == c, x_cross, 0.0))
+        sums[2 * c] = sums[2 * c] - 0.5 * fold(jnp.where(lane // 2 % comps == c, y_cross, 0.0))
     for j in range(2):
         ends = jnp.sum(fold(weights[j] * lack), axis=0, keepdims=True)
         last = jnp.sum(jnp.where(lane == 2 * row, ends, 0.0), axis=1, keepdims=True)
         first = jnp.sum(jnp.where(lane == 2 * row + 1, ends, 0.0), axis=1, keepdims=True)
         more = jnp.where(lane == 0, first, jnp.where(lane == lanes - 1, last, 0.0))
-        more = more + x_lack[1 - j] + edge * x_lack[j]
         tips_ref[j] = tips_ref[j] - 0.5 * more
 
     def lane_of(values):
@@ -231,8 +250,6 @@
     own = lane_of(sums)
     sums_send[0] = own
     sums_recv[0] = own
-    spread(sums_send, sums_recv, 1)
-
     def send_tips(step, _):
         owner = lax.rem(gx + 1 + step, owners)
         for q in range(4):
@@ -252,6 +269,7 @@
         return 0
 
     lax.fori_loop(0, owners, send_tips, 0)
+    spread(sums_send, sums_recv, 1)
 
     @pl.when(gx < owners)
     def _():
@@ -270,15 +288,13 @@
         index = z * comps + c
         ends = pltpu.roll(y_halo[...], lanes - 1 - 2 * index, 1)
         ends = jnp.where((lane == 0) | (lane == lanes - 1), ends, 0.0)
-        ends = ends + jnp.where(row == 0, x_halo[0, pl.ds(index, 1), :], 0.0)
-        ends = ends + jnp.where(row == width - 1, x_halo[1, pl.ds(index, 1), :], 0.0)
         return app[c, z] - 0.5 * ends
 
     def solve_early(z, _):
         o = [orb[c, z] for c in range(comps)]
         local = split_dot([whole_applied(c, z) for c in range(comps)] + o)
         for c in range(comps):
-            app[c, z] = o[c] - local[c]
+            app[c, z] = keep * o[c] - local[c]
             shift[c, z] = local[comps + c]
         return 0
 
@@ -286,7 +302,7 @@
 
     totals = gathered(sums_recv, 1, 2 * comps)
     mean_square = [totals[2 * c + 1] / cells for c in range(comps)]
-    energy = [totals[2 * c] / cells / (mean_square[c] + EPS) for c in range(comps)]
+    energy = [totals[2 * c] / cells / (mean_square[c] + EPS) + sigma for c in range(comps)]
 
     @pl.when(gx < owners)
     def _():
@@ -328,14 +344,26 @@
         lax.fori_loop(1, groups, send, 0)
         carry[lax.rem(gx, owners)] = carry_send[0]
 
-    def solve_late(z, _):
+    def finish(c, z, own, mass):
+        app[c, z] = own
+        to_last, to_first = weighted(own)
+        moments[0, pl.ds(z * comps + c, 1), :] = to_first
+        moments[1, pl.ds(z * comps + c, 1), :] = to_last
+        return mass + fold(own * own)
+
+    def finish_early(z, masses):
+        return tuple(
+            finish(c, z, app[c, z] + energy[c] * shift[c, z], masses[c]) for c in range(comps)
+        )
+
+    def solve_late(z, masses):
         o = [orb[c, z] for c in range(comps)]
         local = split_dot([whole_applied(c, z) - energy[c] * o[c] for c in range(comps)])
-        for c in range(comps):
-            app[c, z] = o[c] - local[c]
-        return 0
-
-    lax.fori_loop(early, levels, solve_late, 0, unroll=2)
+        return tuple(finish(c, z, keep * o[c] - local[c], masses[c]) for c in range(comps))
+
+    masses = lax.fori_loop(0, early, finish_early, (zero,) * comps, unroll=2)
+    masses = list(lax.fori_loop(early, levels, solve_late, masses, unroll=2))
+    square = jnp.sum(weights[1] * weights[1], axis=0, keepdims=True)
 
     @pl.when(gx < owners)
     def _():
@@ -345,31 +373,37 @@
     def _():
         wait_bytes(carry, recv_sem.at[2])
 
-    def update_owner(is_early, owner, masses):
-        masses = list(masses)
+    def join_mass(owner, held):
+        forward, backward = carry[owner, 0:rows, :], carry[owner, rows : 2 * rows, :]
+        here = pl.ds(owner * rows, rows)
+        held = held + forward * (square * forward - 2.0 * moments[0, here, :])
+        held = held + backward * (square * backward - 2.0 * moments[1, here, :])
+        return held + 2.0 * float(width) * edge * forward * backward
+
+    joined = lax.fori_loop(0, owners, join_mass, jnp.zeros((rows, lanes), jnp.float32), unroll=4)
+    line_row = lax.broadcasted_iota(jnp.int32, (rows, lanes), 0)
+    for c in range(comps):
+        more = jnp.sum(jnp.where(line_row % comps == c, joined, 0.0), axis=0, keepdims=True)
+        masses[c] = jnp.sum(masses[c], axis=0, keepdims=True) + more
+    own = lane_of(masses)
+    mass_send[0] = own
+    mass_recv[0] = own
+    spread(mass_send, mass_recv, 3)
+
+    def update_owner(owner, _):
         for local in range(per):
             z = owner * per + local
             for c in range(comps):
                 at = local * comps + c
-                update = app[c, z]
-                if is_early:
-                    update = update + energy[c] * shift[c, z]
-                update = update - (
+                app[c, z] = app[c, z] - (
                     weights[1] * carry[owner, at : at + 1, :]
                     + weights[0] * carry[owner, rows + at : rows + at + 1, :]
                 )
-                app[c, z] = update
-                masses[c] = masses[c] + fold(update * update)
         levels_here = pl.ds(owner * per, per)
         pltpu.make_async_copy(app.at[:, levels_here], out_hbm.at[:, levels_here], out_sem).start()
-        return tuple(masses)
-
-    masses = lax.fori_loop(0, early // per, functools.partial(update_owner, True), (zero,) * comps)
-    masses = lax.fori_loop(early // per, owners, functools.partial(update_owner, False), masses)
-    own = lane_of(masses)
-    mass_send[0] = own
-    mass_recv[0] = own
-    spread(mass_send, mass_recv, 3)
+        return 0
+
+    lax.fori_loop(0, owners, update_owner, 0)
     totals = gathered(mass_recv, 3, comps)
     for c in range(comps):
         ratio = jnp.sqrt(mean_square[c] / (totals[c] / cells + EPS))
@@ -400,21 +434,7 @@
     early = levels // 2
     planes = comps * levels
     devices = groups * columns
-    line_cells = width * groups
-    cells = float(levels * line_cells * lanes * columns)
-    sigma = shift_ratio[0] / float(line_cells * line_cells)
-    decay = jnp.log1p(sigma + jnp.sqrt(sigma * (sigma + 2.0)))
-    gain = TAU * jnp.tanh(0.5 * decay)
-    params = jnp.stack(
-        [
-            decay,
-            gain,
-            gain * jnp.exp(-decay),
-            jnp.exp(-decay * width),
-            -1.0 / jnp.expm1(-decay * line_cells),
-            jnp.exp(-decay * (width - 1)),
-        ]
-    )
+    cells = float(levels * width * groups * lanes * columns)
     f32 = jnp.float32
     update, ratio = pl.pallas_call(
         functools.partial(step_kernel, groups, owners, cells),
@@ -424,8 +444,8 @@
         ),
         in_specs=[
             pl.BlockSpec(memory_space=pltpu.SMEM),
-            pl.BlockSpec(memory_space=pl.ANY),
-            pl.BlockSpec(memory_space=pl.ANY),
+            pl.BlockSpec(memory_space=pltpu.HBM),
+            pl.BlockSpec(memory_space=pltpu.HBM),
         ],
         out_specs=(
             pl.BlockSpec(memory_space=pl.ANY),
@@ -439,10 +459,11 @@
             pltpu.VMEM((width, 3 * width), jnp.bfloat16),
             pltpu.VMEM((2, width, lanes), f32),
             pltpu.VMEM((2, planes, lanes), f32),
-            pltpu.VMEM((2, planes, lanes), f32),
+            pltpu.VMEM((planes, lanes), f32),
             pltpu.VMEM((width, lanes), f32),
             pltpu.VMEM((width, lanes), f32),
             pltpu.VMEM((4, planes, lanes), f32),
+            pltpu.VMEM((2, planes, lanes), f32),
             pltpu.VMEM((owners, 4 * rows, lanes), f32),
             pltpu.VMEM((groups, 4 * rows, lanes), f32),
             pltpu.VMEM((groups, 2 * rows, lanes), f32),
@@ -452,17 +473,17 @@
             pltpu.VMEM((1, 1, lanes), f32),
             pltpu.VMEM((devices, 1, lanes), f32),
             pltpu.SemaphoreType.DMA((CHUNKS + 1,)),
-            pltpu.SemaphoreType.DMA((3,)),
-            pltpu.SemaphoreType.DMA((3,)),
+            pltpu.SemaphoreType.DMA((2,)),
+            pltpu.SemaphoreType.DMA((2,)),
             pltpu.SemaphoreType.DMA((4,)),
             pltpu.SemaphoreType.DMA((4,)),
             pltpu.SemaphoreType.DMA,
         ],
         compiler_params=pltpu.CompilerParams(
-            collective_id=0, has_side_effects=True
+            collective_id=0, has_side_effects=True, vmem_limit_bytes=32 * 1024 * 1024
         ),
         name="power_step",
-    )(params, orbitals, potential)
+    )(shift_ratio, orbitals, potential)
     return update * ratio[:, None, None, :]
 
 

time: 31.3 us -> 31.1 us (level)
  local copies, waits for them, and re-layouts: 0.61 us -> 2.81 us
  other arithmetic: 3.21 us -> 1.62 us
  Pallas kernels: 26.3 us -> 25.8 us
  between operations: 1 us -> 0.67 us
    unnamed x0 -> x4, local copies, waits for them, and re-layouts: none -> 2.81 us
    mul x1, other arithmetic: 3.21 us -> 1.62 us  [shards(): return update * ratio[:, None, None, :]]
    another operation x1 -> x0, local copies, waits for them, and re-layouts: 0.61 us -> none  [shards(): jnp.stack([decay, gain, gain * jnp.exp(-decay), jnp.exp(-decay * width),...]
    pallas_call x1, Pallas kernels: 26.3 us -> 25.8 us  [shards(): pl.pallas_call(functools.partial(step_kernel, groups, owners, cells), out...]
where the time goes in v2:
time: 31.1 us; the launch traced here: 30.9 us
  Pallas kernels  25.8 us (83%)
  local copies, waits for them, and re-layouts  2.81 us (9%)
  other arithmetic  1.62 us (5%)
  between operations  0.67 us (2%)
    pallas_call x1, Pallas kernels, shards(): pl.pallas_call(functools.partial(step_kernel, groups, owners, cells), out...  25.8 us
    unnamed x4, local copies, waits for them, and re-layouts  2.81 us
    mul x1, other arithmetic, shards(): return update * ratio[:, None, None, :]  1.62 us

profile of v2, /device:TPU:0, one launch (start us, length us, event | category | flops | bytes accessed | tf_op | source)
XLA Modules:
  0.0 30.9 jit_solution(17916011372645219775)
XLA Ops:
  0.7 0.0 copy-start
  0.7 1.6 %copy-done = f32[2,32,64,128]{3,2,1,0:T(8,128)S(1)} copy-done((f32[2,32,64,128]{3,2,1,0:T(8,128)S(1)}, f32[2,32,64,128]{3,2,1,0:T(8,128)}, u32[]{:S(2)}) %copy-start) | copy-done | bytes 2097176
  2.2 0.0 copy-start.1
  2.2 1.2 %copy-done.1 = f32[32,64,128]{2,1,0:T(8,128)S(1)} copy-done((f32[32,64,128]{2,1,0:T(8,128)S(1)}, f32[32,64,128]{2,1,0:T(8,128)}, u32[]{:S(2)}) %copy-start.1) | copy-done | bytes 1048600
  3.5 25.8 %power_step.1 = (f32[2,32,64,128]{3,2,1,0:T(8,128)S(1)}, f32[2,128]{1,0:T(2,128)S(1)}) custom-call(f32[1]{0:T(128)S(6)} %copy.4.shift_ratio, f32[2,32,64,128]{3,2,1,0:T(8,128)S(1)} %copy-done, f32[32,64,128]{2,1,0:T(8,128)S(1)} %copy-done.1), custom_call_target="tpu_custom_call" | custom-call | tf_op jit(solution)/shard_map/power_step/pallas_call | solution.py:439
  29.3 1.6 %broadcast_multiply_fusion = f32[2,32,64,128]{3,2,1,0:T(8,128)} fusion(f32[2,32,64,128]{3,2,1,0:T(8,128)S(1)} %get-tuple-element.7, f32[2,128]{1,0:T(2,128)S(1)} %get-tuple-element.8), kind=kLoop, calls=%fused_computation | loop fusion | flops 524288 | bytes 4195328 | tf_op jit(solution)/shard_map/mul | solution.py:487
Async XLA Ops:
  0.7 1.6 %copy-start = (f32[2,32,64,128]{3,2,1,0:T(8,128)S(1)}, f32[2,32,64,128]{3,2,1,0:T(8,128)}, u32[]{:S(2)}) copy-start(f32[2,32,64,128]{3,2,1,0:T(8,128)} %orb_hbm.1) | copy-start | bytes 6291460
  2.2 1.2 %copy-start.1 = (f32[32,64,128]{2,1,0:T(8,128)S(1)}, f32[32,64,128]{2,1,0:T(8,128)}, u32[]{:S(2)}) copy-start(f32[32,64,128]{2,1,0:T(8,128)} %pot_hbm.1) | copy-start | bytes 3145732

commit v3 on v2

--- a/solution.py
+++ b/solution.py
@@ -15,6 +15,7 @@
 MESH = pl.DeviceIdType.MESH
 LANES = 128
 CHUNKS = 4
+GROUP = 4
 
 
 def wait_bytes(ref, sem):
@@ -121,19 +122,27 @@
     low = (green - high.astype(jnp.float32)).astype(jnp.bfloat16)
     table[...] = jnp.where(t_col >= 2 * width, low.astype(jnp.float32), high.astype(jnp.float32)).astype(jnp.bfloat16)
 
-    def pack(z, held):
-        for c in range(comps):
-            plane = orb[c, z]
-            index = z * comps + c
-            held = jnp.where(lane // 2 == index, pltpu.roll(plane, 2 * index + 1, 1), held)
-            x_send[0, pl.ds(index, 1), :] = orb[c, z, width - 1 : width, :]
-            x_send[1, pl.ds(index, 1), :] = orb[c, z, 0:1, :]
+    def groups_of(size, first, last, body, held):
+        return lax.fori_loop(0, (last - first) // size, lambda i, x: body(first + i * size, x), held)
+
+    def pack(start, held):
+        rows_out = []
+        for i in range(GROUP):
+            z = start + i
+            for c in range(comps):
+                plane = orb[c, z]
+                index = z * comps + c
+                held = jnp.where(lane // 2 == index, pltpu.roll(plane, 2 * index + 1, 1), held)
+                rows_out.append((index, plane[width - 1 : width], plane[0:1]))
+        for index, last, first in rows_out:
+            x_send[0, pl.ds(index, 1), :] = last
+            x_send[1, pl.ds(index, 1), :] = first
         return held
 
     held = jnp.zeros((width, lanes), jnp.float32)
     for i in range(CHUNKS):
         loads[i].wait()
-        held = lax.fori_loop(i * chunk, (i + 1) * chunk, pack, held, unroll=4)
+        held = groups_of(GROUP, i * chunk, (i + 1) * chunk, pack, held)
     y_send[...] = held
 
     pl.semaphore_wait(barrier, devices - 1)
@@ -169,7 +178,7 @@
             jnp.sum(to_first * near_first, axis=0, keepdims=True),
         )
 
-    def apply_level(z, sums):
+    def apply_level(z, sums, stores):
         o = [orb[c, z] for c in range(comps)]
         before = lax.rem(z + levels - 1, levels)
         after = lax.rem(z + 1, levels)
@@ -185,17 +194,24 @@
             near = pltpu.roll(mine, 1, 1) + pltpu.roll(mine, lanes - 1, 1)
             near = near + orb[c, before] + orb[c, after]
             applied = (trap + density[c]) * mine - 0.5 * near
-            app[c, z] = applied
-            for i, x in enumerate((applied, mine)):
-                for j, tip in enumerate(weighted(x)):
-                    tips_ref[2 * i + j, pl.ds(z * comps + c, 1), :] = tip
+            stores.append((c, z, applied, [tip for x in (applied, mine) for tip in weighted(x)]))
             along = mine - pltpu.roll(mine, width - 1, 0)
             result.append(sums[2 * c] + fold(mine * (applied + along)))
             result.append(sums[2 * c + 1] + fold(squares[c]))
         return tuple(result)
 
+    def apply_pair(start, sums):
+        stores = []
+        for i in range(2):
+            sums = apply_level(start + i, sums, stores)
+        for c, z, applied, tips in stores:
+            app[c, z] = applied
+            for q, tip in enumerate(tips):
+                tips_ref[q, pl.ds(z * comps + c, 1), :] = tip
+        return sums
+
     zero = jnp.zeros((8, lanes), jnp.float32)
-    sums = list(lax.fori_loop(0, levels, apply_level, (zero,) * (2 * comps), unroll=2))
+    sums = list(groups_of(2, 0, levels, apply_pair, (zero,) * (2 * comps)))
 
     for copy in halos:
         copy.wait()
@@ -290,15 +306,16 @@
         ends = jnp.where((lane == 0) | (lane == lanes - 1), ends, 0.0)
         return app[c, z] - 0.5 * ends
 
-    def solve_early(z, _):
-        o = [orb[c, z] for c in range(comps)]
-        local = split_dot([whole_applied(c, z) for c in range(comps)] + o)
-        for c in range(comps):
-            app[c, z] = keep * o[c] - local[c]
-            shift[c, z] = local[comps + c]
+    def solve_early(start, _):
+        places = [(c, start + i) for i in range(GROUP) for c in range(comps)]
+        o = [orb[c, z] for c, z in places]
+        local = split_dot([whole_applied(c, z) for c, z in places] + o)
+        for i, (c, z) in enumerate(places):
+            app[c, z] = keep * o[i] - local[i]
+            shift[c, z] = local[len(places) + i]
         return 0
 
-    lax.fori_loop(0, early, solve_early, 0, unroll=2)
+    groups_of(GROUP, 0, early, solve_early, 0)
 
     totals = gathered(sums_recv, 1, 2 * comps)
     mean_square = [totals[2 * c + 1] / cells for c in range(comps)]
@@ -318,7 +335,7 @@
             return block * ahead + tips(k), block * behind + tips(groups - 1 - k)
 
         start = jnp.zeros((2 * rows, lanes), jnp.float32)
-        ahead, behind = lax.fori_loop(0, groups, collect, (start, start))
+        ahead, behind = lax.fori_loop(0, groups, collect, (start, start), unroll=4)
 
         def hand_out(k, held):
             ahead, behind = held
@@ -328,7 +345,7 @@
             return block * ahead + tip_gain * tips(k), block * behind + tip_gain * tips(back)
 
         factor = tip_gain * inv_wrap
-        lax.fori_loop(0, groups, hand_out, (factor * ahead, factor * behind))
+        lax.fori_loop(0, groups, hand_out, (factor * ahead, factor * behind), unroll=4)
 
         def send(step, _):
             pltpu.make_async_remote_copy(
@@ -344,25 +361,30 @@
         lax.fori_loop(1, groups, send, 0)
         carry[lax.rem(gx, owners)] = carry_send[0]
 
-    def finish(c, z, own, mass):
-        app[c, z] = own
-        to_last, to_first = weighted(own)
-        moments[0, pl.ds(z * comps + c, 1), :] = to_first
-        moments[1, pl.ds(z * comps + c, 1), :] = to_last
-        return mass + fold(own * own)
-
-    def finish_early(z, masses):
-        return tuple(
-            finish(c, z, app[c, z] + energy[c] * shift[c, z], masses[c]) for c in range(comps)
-        )
-
-    def solve_late(z, masses):
-        o = [orb[c, z] for c in range(comps)]
-        local = split_dot([whole_applied(c, z) - energy[c] * o[c] for c in range(comps)])
-        return tuple(finish(c, z, keep * o[c] - local[c], masses[c]) for c in range(comps))
-
-    masses = lax.fori_loop(0, early, finish_early, (zero,) * comps, unroll=2)
-    masses = list(lax.fori_loop(early, levels, solve_late, masses, unroll=2))
+    def finish(places, fields, masses):
+        masses = list(masses)
+        ends = []
+        for (c, z), own in zip(places, fields):
+            ends.append(weighted(own))
+            masses[c] = masses[c] + fold(own * own)
+        for (c, z), own, (to_last, to_first) in zip(places, fields, ends):
+            app[c, z] = own
+            moments[0, pl.ds(z * comps + c, 1), :] = to_first
+            moments[1, pl.ds(z * comps + c, 1), :] = to_last
+        return tuple(masses)
+
+    def finish_early(start, masses):
+        places = [(c, start + i) for i in range(2) for c in range(comps)]
+        return finish(places, [app[c, z] + energy[c] * shift[c, z] for c, z in places], masses)
+
+    def solve_late(start, masses):
+        places = [(c, start + i) for i in range(GROUP) for c in range(comps)]
+        o = [orb[c, z] for c, z in places]
+        local = split_dot([whole_applied(c, z) - energy[c] * x for (c, z), x in zip(places, o)])
+        return finish(places, [keep * x - y for x, y in zip(o, local)], masses)
+
+    masses = groups_of(2, 0, early, finish_early, (zero,) * comps)
+    masses = list(groups_of(GROUP, early, levels, solve_late, masses))
     square = jnp.sum(weights[1] * weights[1], axis=0, keepdims=True)
 
     @pl.when(gx < owners)
@@ -391,14 +413,17 @@
     spread(mass_send, mass_recv, 3)
 
     def update_owner(owner, _):
-        for local in range(per):
-            z = owner * per + local
-            for c in range(comps):
-                at = local * comps + c
-                app[c, z] = app[c, z] - (
-                    weights[1] * carry[owner, at : at + 1, :]
-                    + weights[0] * carry[owner, rows + at : rows + at + 1, :]
-                )
+        places = [(c, owner * per + local, local * comps + c) for local in range(per) for c in range(comps)]
+        fields = [
+            app[c, z]
+            - (
+                weights[1] * carry[owner, at : at + 1, :]
+                + weights[0] * carry[owner, rows + at : rows + at + 1, :]
+            )
+            for c, z, at in places
+        ]
+        for (c, z, at), field in zip(places, fields):
+            app[c, z] = field
         levels_here = pl.ds(owner * per, per)
         pltpu.make_async_copy(app.at[:, levels_here], out_hbm.at[:, levels_here], out_sem).start()
         return 0
@@ -483,7 +508,11 @@
             collective_id=0, has_side_effects=True, vmem_limit_bytes=32 * 1024 * 1024
         ),
         name="power_step",
-    )(shift_ratio, orbitals, potential)
+    )(
+        shift_ratio,
+        pltpu.with_memory_space_constraint(orbitals, pltpu.HBM),
+        pltpu.with_memory_space_constraint(potential, pltpu.HBM),
+    )
     return update * ratio[:, None, None, :]
 
 

time: 31.1 us -> 28 us (0.900)
  local copies, waits for them, and re-layouts: 2.81 us -> 0 us
    unnamed x4 -> x0, local copies, waits for them, and re-layouts: 2.81 us -> none
where the time goes in v3:
time: 28 us; the launch traced here: 27.8 us
  Pallas kernels  25.5 us (91%)
  other arithmetic  1.62 us (6%)
  between operations  0.66 us (2%)
    pallas_call x1, Pallas kernels, shards(): pl.pallas_call(functools.partial(step_kernel, groups, owners, cells), out...  25.5 us
    mul x1, other arithmetic, shards(): return update * ratio[:, None, None, :]  1.62 us

profile of v3, /device:TPU:0, one launch (start us, length us, event | category | flops | bytes accessed | tf_op | source)
XLA Modules:
  0.0 27.8 jit_solution(3691960417872742803)
XLA Ops:
  0.7 25.5 %power_step.1 = (f32[2,32,64,128]{3,2,1,0:T(8,128)S(1)}, f32[2,128]{1,0:T(2,128)S(1)}) custom-call(f32[1]{0:T(128)S(6)} %copy.4.shift_ratio, f32[2,32,64,128]{3,2,1,0:T(8,128)} %orb_hbm.1, f32[32,64,128]{2,1,0:T(8,128)} %pot_hbm.1), custom_call_target="tpu_custom_call" | custom-call | tf_op jit(solution)/shard_map/power_step/pallas_call | solution.py:464
  26.2 1.6 %broadcast_multiply_fusion = f32[2,32,64,128]{3,2,1,0:T(8,128)} fusion(f32[2,32,64,128]{3,2,1,0:T(8,128)S(1)} %get-tuple-element.7, f32[2,128]{1,0:T(2,128)S(1)} %get-tuple-element.8), kind=kLoop, calls=%fused_computation | loop fusion | flops 524288 | bytes 4195328 | tf_op jit(solution)/shard_map/mul | solution.py:516

commit v4 on v3

--- a/solution.py
+++ b/solution.py
@@ -45,6 +45,8 @@
     moments,
     tip_send,
     tip_recv,
+    orb_tip_send,
+    orb_tip_recv,
     carry_send,
     carry,
     sums_send,
@@ -125,8 +127,36 @@
     def groups_of(size, first, last, body, held):
         return lax.fori_loop(0, (last - first) // size, lambda i, x: body(first + i * size, x), held)
 
+    def weighted(x):
+        parts = [x[i : i + 8] for i in range(0, width, 8)]
+        to_last, to_first = parts[0], parts[-1]
+        for i in range(1, len(parts)):
+            to_last = to_last * eight + parts[i]
+            to_first = to_first * eight + parts[-1 - i]
+        return (
+            jnp.sum(to_last * near_last, axis=0, keepdims=True),
+            jnp.sum(to_first * near_first, axis=0, keepdims=True),
+        )
+
+    def copy_tips(source, target, which, step):
+        def go():
+            pltpu.make_async_remote_copy(
+                source.at[peer(step)],
+                target.at[groups - step],
+                send_sem.at[which],
+                recv_sem.at[which],
+                device_id=device_at(step, 0),
+                device_id_type=MESH,
+            ).start()
+
+        if owners == groups:
+            go()
+        else:
+            pl.when(peer(step) < owners)(go)
+
     def pack(start, held):
         rows_out = []
+        ends = []
         for i in range(GROUP):
             z = start + i
             for c in range(comps):
@@ -134,9 +164,13 @@
                 index = z * comps + c
                 held = jnp.where(lane // 2 == index, pltpu.roll(plane, 2 * index + 1, 1), held)
                 rows_out.append((index, plane[width - 1 : width], plane[0:1]))
+                ends.append((lax.div(start, per) + i // per, i % per * comps + c, weighted(plane)))
         for index, last, first in rows_out:
             x_send[0, pl.ds(index, 1), :] = last
             x_send[1, pl.ds(index, 1), :] = first
+        for owner, at, tips in ends:
+            for j, tip in enumerate(tips):
+                orb_tip_send[owner, j * rows + at : j * rows + at + 1, :] = tip
         return held
 
     held = jnp.zeros((width, lanes), jnp.float32)
@@ -166,17 +200,6 @@
         for i in range(8, width, 8):
             total = total + x[i : i + 8]
         return total
-
-    def weighted(x):
-        parts = [x[i : i + 8] for i in range(0, width, 8)]
-        to_last, to_first = parts[0], parts[-1]
-        for i in range(1, len(parts)):
-            to_last = to_last * eight + parts[i]
-            to_first = to_first * eight + parts[-1 - i]
-        return (
-            jnp.sum(to_last * near_last, axis=0, keepdims=True),
-            jnp.sum(to_first * near_first, axis=0, keepdims=True),
-        )
 
     def apply_level(z, sums, stores):
         o = [orb[c, z] for c in range(comps)]
@@ -194,7 +217,7 @@
             near = pltpu.roll(mine, 1, 1) + pltpu.roll(mine, lanes - 1, 1)
             near = near + orb[c, before] + orb[c, after]
             applied = (trap + density[c]) * mine - 0.5 * near
-            stores.append((c, z, applied, [tip for x in (applied, mine) for tip in weighted(x)]))
+            stores.append((c, z, applied, weighted(applied)))
             along = mine - pltpu.roll(mine, width - 1, 0)
             result.append(sums[2 * c] + fold(mine * (applied + along)))
             result.append(sums[2 * c + 1] + fold(squares[c]))
@@ -211,7 +234,23 @@
         return sums
 
     zero = jnp.zeros((8, lanes), jnp.float32)
-    sums = list(groups_of(2, 0, levels, apply_pair, (zero,) * (2 * comps)))
+    sums = (zero,) * (2 * comps)
+    if owners == groups and levels == 2 * groups:
+
+        def apply_and_send(step, sums):
+            copy_tips(orb_tip_send, orb_tip_recv, 4, step)
+            return apply_pair(2 * step, sums)
+
+        sums = lax.fori_loop(1, groups, apply_and_send, apply_pair(0, sums))
+    else:
+
+        def send_early(step, _):
+            copy_tips(orb_tip_send, orb_tip_recv, 4, step)
+            return 0
+
+        lax.fori_loop(1, groups, send_early, 0)
+        sums = groups_of(2, 0, levels, apply_pair, sums)
+    sums = list(sums)
 
     for copy in halos:
         copy.wait()
@@ -237,24 +276,19 @@
             packed = jnp.where(lane_row == i, whole, packed)
         return packed
 
-    def spread(source, target, which):
-        def copy_to(slot, device):
-            pltpu.make_async_remote_copy(
-                source.at[0],
-                target.at[slot],
-                send_sem.at[which],
-                recv_sem.at[which],
-                device_id=device,
-                device_id_type=MESH,
-            ).start()
-
-        def send(step, _):
-            for side in range(2):
-                copy_to(2 * (groups - step) + side, device_at(step, side))
-            return 0
-
-        copy_to(1, (gx, 1 - gy))
-        lax.fori_loop(1, groups, send, 0)
+    def copy_sums(source, target, which, slot, device):
+        pltpu.make_async_remote_copy(
+            source.at[0],
+            target.at[slot],
+            send_sem.at[which],
+            recv_sem.at[which],
+            device_id=device,
+            device_id_type=MESH,
+        ).start()
+
+    def spread(source, target, which, step):
+        for side in range(2):
+            copy_sums(source, target, which, 2 * (groups - step) + side, device_at(step, side))
 
     def gathered(target, which, count):
         wait_bytes(target.at[pl.ds(1, devices - 1)], recv_sem.at[which])
@@ -266,30 +300,25 @@
     own = lane_of(sums)
     sums_send[0] = own
     sums_recv[0] = own
-    def send_tips(step, _):
-        owner = lax.rem(gx + 1 + step, owners)
-        for q in range(4):
-            tip_send[owner, q * rows : (q + 1) * rows, :] = tips_ref[q, pl.ds(owner * rows, rows), :]
-
-        @pl.when(owner != gx)
-        def _():
-            pltpu.make_async_remote_copy(
-                tip_send.at[owner],
-                tip_recv.at[lax.rem(gx - owner + groups, groups)],
-                send_sem.at[0],
-                recv_sem.at[0],
-                device_id=(owner, gy),
-                device_id_type=MESH,
-            ).start()
-
+    def fill_tips(owner, _):
+        for j in range(2):
+            tip_send[owner, j * rows : (j + 1) * rows, :] = tips_ref[j, pl.ds(owner * rows, rows), :]
         return 0
 
-    lax.fori_loop(0, owners, send_tips, 0)
-    spread(sums_send, sums_recv, 1)
+    lax.fori_loop(0, owners, fill_tips, 0, unroll=4)
+
+    def send_line_ends(step, _):
+        copy_tips(tip_send, tip_recv, 0, step)
+        spread(sums_send, sums_recv, 1, step)
+        return 0
+
+    copy_sums(sums_send, sums_recv, 1, 1, (gx, 1 - gy))
+    lax.fori_loop(1, groups, send_line_ends, 0)
 
     @pl.when(gx < owners)
     def _():
         tip_recv[0] = tip_send[lax.rem(gx, owners)]
+        orb_tip_recv[0] = orb_tip_send[lax.rem(gx, owners)]
 
     def split_dot(fields):
         wide = jnp.concatenate(fields, axis=1)
@@ -324,11 +353,12 @@
     @pl.when(gx < owners)
     def _():
         wait_bytes(tip_recv.at[pl.ds(1, groups - 1)], recv_sem.at[0])
+        wait_bytes(orb_tip_recv.at[pl.ds(1, groups - 1)], recv_sem.at[4])
         tip_row = lax.broadcasted_iota(jnp.int32, (2 * rows, lanes), 0)
         scale = jnp.where(tip_row % 2 == 0, energy[0], energy[1])
 
         def tips(k):
-            return tip_recv[k, 0 : 2 * rows, :] - scale * tip_recv[k, 2 * rows : 4 * rows, :]
+            return tip_recv[k] - scale * orb_tip_recv[k]
 
         def collect(k, held):
             ahead, behind = held
@@ -410,7 +440,13 @@
     own = lane_of(masses)
     mass_send[0] = own
     mass_recv[0] = own
-    spread(mass_send, mass_recv, 3)
+    copy_sums(mass_send, mass_recv, 3, 1, (gx, 1 - gy))
+
+    def send_mass(step, _):
+        spread(mass_send, mass_recv, 3, step)
+        return 0
+
+    lax.fori_loop(1, groups, send_mass, 0)
 
     def update_owner(owner, _):
         places = [(c, owner * per + local, local * comps + c) for local in range(per) for c in range(comps)]
@@ -437,11 +473,13 @@
     @pl.when(gx < owners)
     def _():
         wait_bytes(tip_send.at[pl.ds(0, owners - 1)], send_sem.at[0])
+        wait_bytes(orb_tip_send.at[pl.ds(0, owners - 1)], send_sem.at[4])
         wait_bytes(carry_send.at[pl.ds(1, groups - 1)], send_sem.at[2])
 
     @pl.when(gx >= owners)
     def _():
         wait_bytes(tip_send, send_sem.at[0])
+        wait_bytes(orb_tip_send, send_sem.at[4])
 
     wait_bytes(sums_recv.at[pl.ds(1, devices - 1)], send_sem.at[1])
     wait_bytes(mass_recv.at[pl.ds(1, devices - 1)], send_sem.at[3])
@@ -487,10 +525,12 @@
             pltpu.VMEM((planes, lanes), f32),
             pltpu.VMEM((width, lanes), f32),
             pltpu.VMEM((width, lanes), f32),
-            pltpu.VMEM((4, planes, lanes), f32),
             pltpu.VMEM((2, planes, lanes), f32),
-            pltpu.VMEM((owners, 4 * rows, lanes), f32),
-            pltpu.VMEM((groups, 4 * rows, lanes), f32),
+            pltpu.VMEM((2, planes, lanes), f32),
+            pltpu.VMEM((owners, 2 * rows, lanes), f32),
+            pltpu.VMEM((groups, 2 * rows, lanes), f32),
+            pltpu.VMEM((owners, 2 * rows, lanes), f32),
+            pltpu.VMEM((groups, 2 * rows, lanes), f32),
             pltpu.VMEM((groups, 2 * rows, lanes), f32),
             pltpu.VMEM((owners, 2 * rows, lanes), f32),
             pltpu.VMEM((1, 1, lanes), f32),
@@ -500,8 +540,8 @@
             pltpu.SemaphoreType.DMA((CHUNKS + 1,)),
             pltpu.SemaphoreType.DMA((2,)),
             pltpu.SemaphoreType.DMA((2,)),
-            pltpu.SemaphoreType.DMA((4,)),
-            pltpu.SemaphoreType.DMA((4,)),
+            pltpu.SemaphoreType.DMA((5,)),
+            pltpu.SemaphoreType.DMA((5,)),
             pltpu.SemaphoreType.DMA,
         ],
         compiler_params=pltpu.CompilerParams(

time: 28 us -> 27.1 us (0.968)
  Pallas kernels: 25.5 us -> 24.6 us
    pallas_call x1, Pallas kernels: 25.5 us -> 24.6 us  [shards(): pl.pallas_call(functools.partial(step_kernel, groups, owners, cells), out...]
where the time goes in v4:
time: 27.1 us; the launch traced here: 26.9 us
  Pallas kernels  24.6 us (91%)
  other arithmetic  1.62 us (6%)
  between operations  0.66 us (2%)
    pallas_call x1, Pallas kernels, shards(): pl.pallas_call(functools.partial(step_kernel, groups, owners, cells), out...  24.6 us
    mul x1, other arithmetic, shards(): return update * ratio[:, None, None, :]  1.62 us

profile of v4, /device:TPU:0, one launch (start us, length us, event | category | flops | bytes accessed | tf_op | source)
XLA Modules:
  0.0 26.9 jit_solution(12875722432000688764)
XLA Ops:
  0.7 24.6 %power_step.1 = (f32[2,32,64,128]{3,2,1,0:T(8,128)S(1)}, f32[2,128]{1,0:T(2,128)S(1)}) custom-call(f32[1]{0:T(128)S(6)} %copy.4.shift_ratio, f32[2,32,64,128]{3,2,1,0:T(8,128)} %orb_hbm.1, f32[32,64,128]{2,1,0:T(8,128)} %pot_hbm.1), custom_call_target="tpu_custom_call" | custom-call | tf_op jit(solution)/shard_map/power_step/pallas_call | solution.py:502
  25.3 1.6 %broadcast_multiply_fusion = f32[2,32,64,128]{3,2,1,0:T(8,128)} fusion(f32[2,32,64,128]{3,2,1,0:T(8,128)S(1)} %get-tuple-element.7, f32[2,128]{1,0:T(2,128)S(1)} %get-tuple-element.8), kind=kLoop, calls=%fused_computation | loop fusion | flops 524288 | bytes 4195328 | tf_op jit(solution)/shard_map/mul | solution.py:556

commit v5 on v4

--- a/solution.py
+++ b/solution.py
@@ -69,6 +69,8 @@
     gy = lax.axis_index("gy")
     lane = lax.broadcasted_iota(jnp.int32, (width, lanes), 1)
     row = lax.broadcasted_iota(jnp.int32, (width, lanes), 0)
+    plane_of = lax.shift_right_logical(lane, 1)
+    odd_lane = lane & 1
     lane_row = lax.broadcasted_iota(jnp.int32, (1, lanes), 1)
 
     def peer(step):
@@ -97,7 +99,7 @@
         return 0
 
     pl.semaphore_signal(barrier, inc=1, device_id=(gx, 1 - gy), device_id_type=MESH)
-    lax.fori_loop(1, groups, greet, 0)
+    lax.fori_loop(1, groups, greet, 0, unroll=3)
 
     line_cells = width * groups
     sigma_wide = jnp.full((1, 2 * lanes), shift_ratio[0] / float(line_cells * line_cells), jnp.float32)
@@ -162,7 +164,7 @@
             for c in range(comps):
                 plane = orb[c, z]
                 index = z * comps + c
-                held = jnp.where(lane // 2 == index, pltpu.roll(plane, 2 * index + 1, 1), held)
+                held = jnp.where(plane_of == index, pltpu.roll(plane, 2 * index + 1, 1), held)
                 rows_out.append((index, plane[width - 1 : width], plane[0:1]))
                 ends.append((lax.div(start, per) + i // per, i % per * comps + c, weighted(plane)))
         for index, last, first in rows_out:
@@ -255,17 +257,17 @@
     for copy in halos:
         copy.wait()
     lack = y_halo[...] - y_send[...]
-    lack = jnp.where(lane % 2 == 0, pltpu.roll(lack, lanes - 1, 1), pltpu.roll(lack, 1, 1))
+    lack = jnp.where(odd_lane == 0, pltpu.roll(lack, lanes - 1, 1), pltpu.roll(lack, 1, 1))
     y_halo[...] = lack
     x_cross = x_send[0] * (x_halo[...] - x_send[1])
     y_cross = y_send[...] * lack
     for c in range(comps):
-        sums[2 * c] = sums[2 * c] - fold(jnp.where(row % comps == c, x_cross, 0.0))
-        sums[2 * c] = sums[2 * c] - 0.5 * fold(jnp.where(lane // 2 % comps == c, y_cross, 0.0))
+        sums[2 * c] = sums[2 * c] - fold(jnp.where((row & 1) == c, x_cross, 0.0))
+        sums[2 * c] = sums[2 * c] - 0.5 * fold(jnp.where((plane_of & 1) == c, y_cross, 0.0))
     for j in range(2):
         ends = jnp.sum(fold(weights[j] * lack), axis=0, keepdims=True)
-        last = jnp.sum(jnp.where(lane == 2 * row, ends, 0.0), axis=1, keepdims=True)
-        first = jnp.sum(jnp.where(lane == 2 * row + 1, ends, 0.0), axis=1, keepdims=True)
+        last = jnp.sum(jnp.where((plane_of == row) & (odd_lane == 0), ends, 0.0), axis=1, keepdims=True)
+        first = jnp.sum(jnp.where((plane_of == row) & (odd_lane == 1), ends, 0.0), axis=1, keepdims=True)
         more = jnp.where(lane == 0, first, jnp.where(lane == lanes - 1, last, 0.0))
         tips_ref[j] = tips_ref[j] - 0.5 * more
 
@@ -313,7 +315,7 @@
         return 0
 
     copy_sums(sums_send, sums_recv, 1, 1, (gx, 1 - gy))
-    lax.fori_loop(1, groups, send_line_ends, 0)
+    lax.fori_loop(1, groups, send_line_ends, 0, unroll=3)
 
     @pl.when(gx < owners)
     def _():
@@ -329,11 +331,11 @@
         )
         return [local[:, i * lanes : (i + 1) * lanes] for i in range(len(fields))]
 
+    side = jnp.where((lane == 0) | (lane == lanes - 1), -0.5, 0.0)
+
     def whole_applied(c, z):
         index = z * comps + c
-        ends = pltpu.roll(y_halo[...], lanes - 1 - 2 * index, 1)
-        ends = jnp.where((lane == 0) | (lane == lanes - 1), ends, 0.0)
-        return app[c, z] - 0.5 * ends
+        return app[c, z] + side * pltpu.roll(y_halo[...], lanes - 1 - 2 * index, 1)
 
     def solve_early(start, _):
         places = [(c, start + i) for i in range(GROUP) for c in range(comps)]
@@ -355,7 +357,7 @@
         wait_bytes(tip_recv.at[pl.ds(1, groups - 1)], recv_sem.at[0])
         wait_bytes(orb_tip_recv.at[pl.ds(1, groups - 1)], recv_sem.at[4])
         tip_row = lax.broadcasted_iota(jnp.int32, (2 * rows, lanes), 0)
-        scale = jnp.where(tip_row % 2 == 0, energy[0], energy[1])
+        scale = jnp.where((tip_row & 1) == 0, energy[0], energy[1])
 
         def tips(k):
             return tip_recv[k] - scale * orb_tip_recv[k]
@@ -388,7 +390,7 @@
             ).start()
             return 0
 
-        lax.fori_loop(1, groups, send, 0)
+        lax.fori_loop(1, groups, send, 0, unroll=3)
         carry[lax.rem(gx, owners)] = carry_send[0]
 
     def finish(places, fields, masses):
@@ -435,7 +437,7 @@
     joined = lax.fori_loop(0, owners, join_mass, jnp.zeros((rows, lanes), jnp.float32), unroll=4)
     line_row = lax.broadcasted_iota(jnp.int32, (rows, lanes), 0)
     for c in range(comps):
-        more = jnp.sum(jnp.where(line_row % comps == c, joined, 0.0), axis=0, keepdims=True)
+        more = jnp.sum(jnp.where((line_row & 1) == c, joined, 0.0), axis=0, keepdims=True)
         masses[c] = jnp.sum(masses[c], axis=0, keepdims=True) + more
     own = lane_of(masses)
     mass_send[0] = own
@@ -446,7 +448,7 @@
         spread(mass_send, mass_recv, 3, step)
         return 0
 
-    lax.fori_loop(1, groups, send_mass, 0)
+    lax.fori_loop(1, groups, send_mass, 0, unroll=3)
 
     def update_owner(owner, _):
         places = [(c, owner * per + local, local * comps + c) for local in range(per) for c in range(comps)]
@@ -491,7 +493,7 @@
     columns = lax.axis_size("gy")
     comps, levels, width, lanes = orbitals.shape
     assert columns == 2 and lanes == LANES and 2 * comps * levels == lanes
-    assert comps * levels == width
+    assert comps == 2 and comps * levels == width
     owners = min(groups, levels)
     rows = comps * (levels // owners)
     early = levels // 2

time: 27.1 us -> 27 us (level)
  no operation moved by 1% of the time
where the time goes in v5:
time: 27 us; the launch traced here: 26.9 us
  Pallas kernels  24.6 us (91%)
  other arithmetic  1.62 us (6%)
  between operations  0.66 us (2%)
    pallas_call x1, Pallas kernels, shards(): pl.pallas_call(functools.partial(step_kernel, groups, owners, cells), out...  24.6 us
    mul x1, other arithmetic, shards(): return update * ratio[:, None, None, :]  1.62 us

profile of v5, /device:TPU:0, one launch (start us, length us, event | category | flops | bytes accessed | tf_op | source)
XLA Modules:
  0.0 26.9 jit_solution(3687939594695336564)
XLA Ops:
  0.7 24.6 %power_step.1 = (f32[2,32,64,128]{3,2,1,0:T(8,128)S(1)}, f32[2,128]{1,0:T(2,128)S(1)}) custom-call(f32[1]{0:T(128)S(6)} %copy.4.shift_ratio, f32[2,32,64,128]{3,2,1,0:T(8,128)} %orb_hbm.1, f32[32,64,128]{2,1,0:T(8,128)} %pot_hbm.1), custom_call_target="tpu_custom_call" | custom-call | tf_op jit(solution)/shard_map/power_step/pallas_call | solution.py:504
  25.3 1.6 %broadcast_multiply_fusion = f32[2,32,64,128]{3,2,1,0:T(8,128)} fusion(f32[2,32,64,128]{3,2,1,0:T(8,128)S(1)} %get-tuple-element.7, f32[2,128]{1,0:T(2,128)S(1)} %get-tuple-element.8), kind=kLoop, calls=%fused_computation | loop fusion | flops 524288 | bytes 4195328 | tf_op jit(solution)/shard_map/mul | solution.py:558

commit v6 on v5

--- a/solution.py
+++ b/solution.py
@@ -49,10 +49,10 @@
     orb_tip_recv,
     carry_send,
     carry,
-    sums_send,
-    sums_recv,
-    mass_send,
-    mass_recv,
+    sums_near,
+    sums_far,
+    mass_near,
+    mass_far,
     load_sem,
     halo_send_sem,
     halo_recv_sem,
@@ -64,7 +64,6 @@
     per = levels // owners
     early = shift.shape[1]
     rows = comps * per
-    devices = 2 * groups
     gx = lax.axis_index("gx")
     gy = lax.axis_index("gy")
     lane = lax.broadcasted_iota(jnp.int32, (width, lanes), 1)
@@ -77,8 +76,16 @@
         other = gx + step
         return jnp.where(other >= groups, other - groups, other)
 
-    def device_at(step, side):
-        return (peer(step), gy if side == 0 else 1 - gy)
+    pairs = groups // 2
+    core = lax.rem(gx, 2)
+
+    def near_device(code):
+        other = gx + 1 - 2 * core if code % 2 else gx
+        return (other, 1 - gy if code >= 2 else gy)
+
+    def far_device(step):
+        other = lax.div(gx, 2) + step
+        return (2 * jnp.where(other >= pairs, other - pairs, other) + core, gy)
 
     chunk = levels // CHUNKS
     loads = [
@@ -94,11 +101,11 @@
     barrier = pltpu.get_barrier_semaphore()
 
     def greet(step, _):
-        for side in range(2):
-            pl.semaphore_signal(barrier, inc=1, device_id=device_at(step, side), device_id_type=MESH)
+        pl.semaphore_signal(barrier, inc=1, device_id=(peer(step), gy), device_id_type=MESH)
         return 0
 
-    pl.semaphore_signal(barrier, inc=1, device_id=(gx, 1 - gy), device_id_type=MESH)
+    for code in (2, 3):
+        pl.semaphore_signal(barrier, inc=1, device_id=near_device(code), device_id_type=MESH)
     lax.fori_loop(1, groups, greet, 0, unroll=3)
 
     line_cells = width * groups
@@ -147,7 +154,7 @@
                 target.at[groups - step],
                 send_sem.at[which],
                 recv_sem.at[which],
-                device_id=device_at(step, 0),
+                device_id=(peer(step), gy),
                 device_id_type=MESH,
             ).start()
 
@@ -181,7 +188,7 @@
         held = groups_of(GROUP, i * chunk, (i + 1) * chunk, pack, held)
     y_send[...] = held
 
-    pl.semaphore_wait(barrier, devices - 1)
+    pl.semaphore_wait(barrier, groups + 1)
     halos = [
         pltpu.make_async_remote_copy(
             src, dst, halo_send_sem.at[i], halo_recv_sem.at[i], device_id=target, device_id_type=MESH
@@ -278,30 +285,40 @@
             packed = jnp.where(lane_row == i, whole, packed)
         return packed
 
-    def copy_sums(source, target, which, slot, device):
+    def send_row(ref, here, there, which, device):
         pltpu.make_async_remote_copy(
-            source.at[0],
-            target.at[slot],
+            ref.at[here],
+            ref.at[there],
             send_sem.at[which],
             recv_sem.at[which],
             device_id=device,
             device_id_type=MESH,
         ).start()
 
-    def spread(source, target, which, step):
-        for side in range(2):
-            copy_sums(source, target, which, 2 * (groups - step) + side, device_at(step, side))
-
-    def gathered(target, which, count):
-        wait_bytes(target.at[pl.ds(1, devices - 1)], recv_sem.at[which])
-        total = jnp.sum(target[...], axis=0)
+    def spread_near(values, near, which):
+        near[0] = lane_of(values)
+        for code in range(1, 4):
+            send_row(near, 0, code, which, near_device(code))
+
+    def spread_far(near, near_which, far, which):
+        wait_bytes(near.at[pl.ds(1, 3)], recv_sem.at[near_which])
+        far[0] = jnp.sum(near[...], axis=0)
+
+        def send(step, _):
+            send_row(far, 0, pairs - step, which, far_device(step))
+            return 0
+
+        lax.fori_loop(1, pairs, send, 0, unroll=7)
+
+    def gathered(far, which, count):
+        wait_bytes(far.at[pl.ds(1, pairs - 1)], recv_sem.at[which])
+        total = jnp.sum(far[...], axis=0)
         return [
             jnp.sum(jnp.where(lane_row == i, total, 0.0), axis=1, keepdims=True) for i in range(count)
         ]
 
-    own = lane_of(sums)
-    sums_send[0] = own
-    sums_recv[0] = own
+    spread_near(sums, sums_near, 1)
+
     def fill_tips(owner, _):
         for j in range(2):
             tip_send[owner, j * rows : (j + 1) * rows, :] = tips_ref[j, pl.ds(owner * rows, rows), :]
@@ -309,13 +326,12 @@
 
     lax.fori_loop(0, owners, fill_tips, 0, unroll=4)
 
-    def send_line_ends(step, _):
+    def send_tips(step, _):
         copy_tips(tip_send, tip_recv, 0, step)
-        spread(sums_send, sums_recv, 1, step)
         return 0
 
-    copy_sums(sums_send, sums_recv, 1, 1, (gx, 1 - gy))
-    lax.fori_loop(1, groups, send_line_ends, 0, unroll=3)
+    lax.fori_loop(1, groups, send_tips, 0, unroll=3)
+    spread_far(sums_near, 1, sums_far, 5)
 
     @pl.when(gx < owners)
     def _():
@@ -348,7 +364,7 @@
 
     groups_of(GROUP, 0, early, solve_early, 0)
 
-    totals = gathered(sums_recv, 1, 2 * comps)
+    totals = gathered(sums_far, 5, 2 * comps)
     mean_square = [totals[2 * c + 1] / cells for c in range(comps)]
     energy = [totals[2 * c] / cells / (mean_square[c] + EPS) + sigma for c in range(comps)]
 
@@ -439,16 +455,7 @@
     for c in range(comps):
         more = jnp.sum(jnp.where((line_row & 1) == c, joined, 0.0), axis=0, keepdims=True)
         masses[c] = jnp.sum(masses[c], axis=0, keepdims=True) + more
-    own = lane_of(masses)
-    mass_send[0] = own
-    mass_recv[0] = own
-    copy_sums(mass_send, mass_recv, 3, 1, (gx, 1 - gy))
-
-    def send_mass(step, _):
-        spread(mass_send, mass_recv, 3, step)
-        return 0
-
-    lax.fori_loop(1, groups, send_mass, 0, unroll=3)
+    spread_near(masses, mass_near, 3)
 
     def update_owner(owner, _):
         places = [(c, owner * per + local, local * comps + c) for local in range(per) for c in range(comps)]
@@ -466,8 +473,10 @@
         pltpu.make_async_copy(app.at[:, levels_here], out_hbm.at[:, levels_here], out_sem).start()
         return 0
 
-    lax.fori_loop(0, owners, update_owner, 0)
-    totals = gathered(mass_recv, 3, comps)
+    lax.fori_loop(0, owners // 2, update_owner, 0)
+    spread_far(mass_near, 3, mass_far, 6)
+    lax.fori_loop(owners // 2, owners, update_owner, 0)
+    totals = gathered(mass_far, 6, comps)
     for c in range(comps):
         ratio = jnp.sqrt(mean_square[c] / (totals[c] / cells + EPS))
         ratio_ref[c : c + 1, :] = jnp.broadcast_to(ratio, (1, lanes))
@@ -483,8 +492,9 @@
         wait_bytes(tip_send, send_sem.at[0])
         wait_bytes(orb_tip_send, send_sem.at[4])
 
-    wait_bytes(sums_recv.at[pl.ds(1, devices - 1)], send_sem.at[1])
-    wait_bytes(mass_recv.at[pl.ds(1, devices - 1)], send_sem.at[3])
+    for near, far, near_which, far_which in ((sums_near, sums_far, 1, 5), (mass_near, mass_far, 3, 6)):
+        wait_bytes(near.at[pl.ds(1, 3)], send_sem.at[near_which])
+        wait_bytes(far.at[pl.ds(1, pairs - 1)], send_sem.at[far_which])
     pltpu.make_async_copy(app, out_hbm, out_sem).wait()
 
 
@@ -498,7 +508,6 @@
     rows = comps * (levels // owners)
     early = levels // 2
     planes = comps * levels
-    devices = groups * columns
     cells = float(levels * width * groups * lanes * columns)
     f32 = jnp.float32
     update, ratio = pl.pallas_call(
@@ -535,15 +544,15 @@
             pltpu.VMEM((groups, 2 * rows, lanes), f32),
             pltpu.VMEM((groups, 2 * rows, lanes), f32),
             pltpu.VMEM((owners, 2 * rows, lanes), f32),
-            pltpu.VMEM((1, 1, lanes), f32),
-            pltpu.VMEM((devices, 1, lanes), f32),
-            pltpu.VMEM((1, 1, lanes), f32),
-            pltpu.VMEM((devices, 1, lanes), f32),
+            pltpu.VMEM((4, 1, lanes), f32),
+            pltpu.VMEM((groups // 2, 1, lanes), f32),
+            pltpu.VMEM((4, 1, lanes), f32),
+            pltpu.VMEM((groups // 2, 1, lanes), f32),
             pltpu.SemaphoreType.DMA((CHUNKS + 1,)),
             pltpu.SemaphoreType.DMA((2,)),
             pltpu.SemaphoreType.DMA((2,)),
-            pltpu.SemaphoreType.DMA((5,)),
-            pltpu.SemaphoreType.DMA((5,)),
+            pltpu.SemaphoreType.DMA((7,)),
+            pltpu.SemaphoreType.DMA((7,)),
             pltpu.SemaphoreType.DMA,
         ],
         compiler_params=pltpu.CompilerParams(

time: 27 us -> 30.1 us (1.11)
  Pallas kernels: 24.6 us -> 27.7 us
    pallas_call x1, Pallas kernels: 24.6 us -> 27.7 us  [shards(): pl.pallas_call(functools.partial(step_kernel, groups, owners, cells), out...]
where the time goes in v6:
time: 30.1 us; the launch traced here: 30 us
  Pallas kernels  27.7 us (92%)
  other arithmetic  1.62 us (5%)
  between operations  0.66 us (2%)
    pallas_call x1, Pallas kernels, shards(): pl.pallas_call(functools.partial(step_kernel, groups, owners, cells), out...  27.7 us
    mul x1, other arithmetic, shards(): return update * ratio[:, None, None, :]  1.62 us

profile of v6, /device:TPU:0, one launch (start us, length us, event | category | flops | bytes accessed | tf_op | source)
XLA Modules:
  0.0 30.0 jit_solution(5314863016167220666)
XLA Ops:
  0.7 27.7 %power_step.1 = (f32[2,32,64,128]{3,2,1,0:T(8,128)S(1)}, f32[2,128]{1,0:T(2,128)S(1)}) custom-call(f32[1]{0:T(128)S(6)} %copy.4.shift_ratio, f32[2,32,64,128]{3,2,1,0:T(8,128)} %orb_hbm.1, f32[32,64,128]{2,1,0:T(8,128)} %pot_hbm.1), custom_call_target="tpu_custom_call" | custom-call | tf_op jit(solution)/shard_map/power_step/pallas_call | solution.py:513
  28.4 1.6 %broadcast_multiply_fusion = f32[2,32,64,128]{3,2,1,0:T(8,128)} fusion(f32[2,32,64,128]{3,2,1,0:T(8,128)S(1)} %get-tuple-element.7, f32[2,128]{1,0:T(2,128)S(1)} %get-tuple-element.8), kind=kLoop, calls=%fused_computation | loop fusion | flops 524288 | bytes 4195328 | tf_op jit(solution)/shard_map/mul | solution.py:567

commit v7 on v4

--- a/solution.py
+++ b/solution.py
@@ -16,6 +16,7 @@
 LANES = 128
 CHUNKS = 4
 GROUP = 4
+SCALE_PARTS = 4
 
 
 def wait_bytes(ref, sem):
@@ -484,6 +485,17 @@
     wait_bytes(sums_recv.at[pl.ds(1, devices - 1)], send_sem.at[1])
     wait_bytes(mass_recv.at[pl.ds(1, devices - 1)], send_sem.at[3])
     pltpu.make_async_copy(app, out_hbm, out_sem).wait()
+
+
+def scale_kernel(update, ratio, out_hbm, stage, sem):
+    comps, levels = update.shape[:2]
+    part = levels // SCALE_PARTS
+    for c in range(comps):
+        for i in range(SCALE_PARTS):
+            here = pl.ds(i * part, part)
+            stage[c, here] = update[c, here] * ratio[c : c + 1, :]
+            pltpu.make_async_copy(stage.at[c, here], out_hbm.at[c, here], sem).start()
+    pltpu.make_async_copy(stage, out_hbm, sem).wait()
 
 
 def shards(orbitals, potential, shift_ratio):
@@ -553,7 +565,18 @@
         pltpu.with_memory_space_constraint(orbitals, pltpu.HBM),
         pltpu.with_memory_space_constraint(potential, pltpu.HBM),
     )
-    return update * ratio[:, None, None, :]
+    return pl.pallas_call(
+        scale_kernel,
+        out_shape=jax.ShapeDtypeStruct(orbitals.shape, f32),
+        in_specs=[pl.BlockSpec(memory_space=pltpu.VMEM), pl.BlockSpec(memory_space=pltpu.VMEM)],
+        out_specs=pl.BlockSpec(memory_space=pl.ANY),
+        scratch_shapes=[pltpu.VMEM(orbitals.shape, f32), pltpu.SemaphoreType.DMA],
+        compiler_params=pltpu.CompilerParams(vmem_limit_bytes=32 * 1024 * 1024),
+        name="scale",
+    )(
+        pltpu.with_memory_space_constraint(update, pltpu.VMEM),
+        pltpu.with_memory_space_constraint(ratio, pltpu.VMEM),
+    )
 
 
 def solution(mesh):

time: 27.1 us -> 26.8 us (0.989)
  other arithmetic: 1.62 us -> 0 us
  Pallas kernels: 24.6 us -> 26 us
    mul x1 -> x0, other arithmetic: 1.62 us -> none  [shards(): return update * ratio[:, None, None, :]]
    pallas_call x0 -> x1, Pallas kernels: none -> 1.33 us  [shards(): pl.pallas_call(scale_kernel, out_shape=jax.ShapeDtypeStruct(orbitals.shap...]
where the time goes in v7:
time: 26.8 us; the launch traced here: 26.6 us
  Pallas kernels  26 us (97%)
  between operations  0.66 us (2%)
    pallas_call x1, Pallas kernels, shards(): pl.pallas_call(functools.partial(step_kernel, groups, owners, cells), out...  24.6 us
    pallas_call x1, Pallas kernels, shards(): pl.pallas_call(scale_kernel, out_shape=jax.ShapeDtypeStruct(orbitals.shap...  1.33 us

profile of v7, /device:TPU:0, one launch (start us, length us, event | category | flops | bytes accessed | tf_op | source)
XLA Modules:
  0.0 26.6 jit_solution(7493649253737100751)
XLA Ops:
  0.7 24.6 %power_step.1 = (f32[2,32,64,128]{3,2,1,0:T(8,128)S(1)}, f32[2,128]{1,0:T(2,128)S(1)}) custom-call(f32[1]{0:T(128)S(6)} %copy.4.shift_ratio, f32[2,32,64,128]{3,2,1,0:T(8,128)} %orb_hbm.1, f32[32,64,128]{2,1,0:T(8,128)} %pot_hbm.1), custom_call_target="tpu_custom_call" | custom-call | tf_op jit(solution)/shard_map/power_step/pallas_call | solution.py:514
  25.3 1.3 %scale.1 = f32[2,32,64,128]{3,2,1,0:T(8,128)} custom-call(f32[2,32,64,128]{3,2,1,0:T(8,128)S(1)} %get-tuple-element.7.update, f32[2,128]{1,0:T(2,128)S(1)} %get-tuple-element.8.ratio), custom_call_target="tpu_custom_call" | custom-call | tf_op jit(solution)/shard_map/scale/pallas_call | solution.py:568

commit v8 on v7

--- a/solution.py
+++ b/solution.py
@@ -506,7 +506,7 @@
     assert comps * levels == width
     owners = min(groups, levels)
     rows = comps * (levels // owners)
-    early = levels // 2
+    early = levels // 4
     planes = comps * levels
     devices = groups * columns
     cells = float(levels * width * groups * lanes * columns)

time: 26.8 us -> 26.8 us (level)
  no operation moved by 1% of the time
where the time goes in v8:
time: 26.8 us; the launch traced here: 26.6 us
  Pallas kernels  26 us (97%)
  between operations  0.66 us (2%)
    pallas_call x1, Pallas kernels, shards(): pl.pallas_call(functools.partial(step_kernel, groups, owners, cells), out...  24.6 us
    pallas_call x1, Pallas kernels, shards(): pl.pallas_call(scale_kernel, out_shape=jax.ShapeDtypeStruct(orbitals.shap...  1.33 us

profile of v8, /device:TPU:0, one launch (start us, length us, event | category | flops | bytes accessed | tf_op | source)
XLA Modules:
  0.0 26.6 jit_solution(14043307695796347168)
XLA Ops:
  0.7 24.6 %power_step.1 = (f32[2,32,64,128]{3,2,1,0:T(8,128)S(1)}, f32[2,128]{1,0:T(2,128)S(1)}) custom-call(f32[1]{0:T(128)S(6)} %copy.4.shift_ratio, f32[2,32,64,128]{3,2,1,0:T(8,128)} %orb_hbm.1, f32[32,64,128]{2,1,0:T(8,128)} %pot_hbm.1), custom_call_target="tpu_custom_call" | custom-call | tf_op jit(solution)/shard_map/power_step/pallas_call | solution.py:514
  25.3 1.3 %scale.1 = f32[2,32,64,128]{3,2,1,0:T(8,128)} custom-call(f32[2,32,64,128]{3,2,1,0:T(8,128)S(1)} %get-tuple-element.7.update, f32[2,128]{1,0:T(2,128)S(1)} %get-tuple-element.8.ratio), custom_call_target="tpu_custom_call" | custom-call | tf_op jit(solution)/shard_map/scale/pallas_call | solution.py:568

commit v9 on v7

--- a/solution.py
+++ b/solution.py
@@ -14,7 +14,7 @@
 COUPLING_CROSS = 0.04
 MESH = pl.DeviceIdType.MESH
 LANES = 128
-CHUNKS = 4
+CHUNKS = 8
 GROUP = 4
 SCALE_PARTS = 4
 

time: 26.8 us -> 26.8 us (level)
  no operation moved by 1% of the time
where the time goes in v9:
time: 26.8 us; the launch traced here: 26.7 us
  Pallas kernels  26 us (97%)
  between operations  0.66 us (2%)
    pallas_call x1, Pallas kernels, shards(): pl.pallas_call(functools.partial(step_kernel, groups, owners, cells), out...  24.7 us
    pallas_call x1, Pallas kernels, shards(): pl.pallas_call(scale_kernel, out_shape=jax.ShapeDtypeStruct(orbitals.shap...  1.33 us

profile of v9, /device:TPU:0, one launch (start us, length us, event | category | flops | bytes accessed | tf_op | source)
XLA Modules:
  0.0 26.7 jit_solution(3568143070418250387)
XLA Ops:
  0.7 24.7 %power_step.1 = (f32[2,32,64,128]{3,2,1,0:T(8,128)S(1)}, f32[2,128]{1,0:T(2,128)S(1)}) custom-call(f32[1]{0:T(128)S(6)} %copy.4.shift_ratio, f32[2,32,64,128]{3,2,1,0:T(8,128)} %orb_hbm.1, f32[32,64,128]{2,1,0:T(8,128)} %pot_hbm.1), custom_call_target="tpu_custom_call" | custom-call | tf_op jit(solution)/shard_map/power_step/pallas_call | solution.py:514
  25.3 1.3 %scale.1 = f32[2,32,64,128]{3,2,1,0:T(8,128)} custom-call(f32[2,32,64,128]{3,2,1,0:T(8,128)S(1)} %get-tuple-element.7.update, f32[2,128]{1,0:T(2,128)S(1)} %get-tuple-element.8.ratio), custom_call_target="tpu_custom_call" | custom-call | tf_op jit(solution)/shard_map/scale/pallas_call | solution.py:568
